TPU v7x, 512 devices: a whole 4x8x8 slice. The times are simulated.
512 devices in a mesh: fsdp: 64 (over y, x, core), dp: 8 (over z).
Axes of the slice: x: 4, y: 8, z: 8, core: 2. Of those that a mesh axis runs over, the one named last changes fastest.
Arguments:
- grads: bfloat16 [8, 64, 1024, 1024], P('dp', None, 'fsdp'), may hold values from -7 to 7
- assign: int32 [64], replicated, may hold values from 0 to 63, each once
- left_factor: float32 [64, 1024, 1024], P('fsdp', 'dp'), may hold values from -1 to 4, as said below
- right_factor: float32 [64, 1024, 1024], P('fsdp', 'dp'), may hold values from -1 to 4, as said below
- left_root: bfloat16 [64, 1024, 1024], P('fsdp', 'dp'), may hold values from -1 to 3, as said below
- right_root: bfloat16 [64, 1024, 1024], P('fsdp', 'dp'), may hold values from -1 to 3, as said below
Outputs:
- update: bfloat16 [64, 1024, 1024], P(None, 'fsdp', 'dp')
- left_new: float32 [64, 1024, 1024], P('fsdp', 'dp')
- right_new: float32 [64, 1024, 1024], P('fsdp', 'dp')
Inputs may be any that keep to these rules, and one draw needn't show every extreme that they name: `assign`: a permutation: each owner holds exactly one block. `left_factor`: each owner's matrix is symmetric. `right_factor`: each owner's matrix is symmetric. `left_root`: each owner's matrix is symmetric. `right_root`: each owner's matrix is symmetric.
All inputs are finite; a program needn't handle non-finite values.
Results may differ from a plain program's by a relative error of at most 0.001.
Values may be sent and summed in bfloat16 or wider, within the bound.
No kernel may reach another device: no remote copies, remote signals or barrier semaphores. Data moves between devices by JAX's collectives and lax.ppermute only.
A program may use at most 64 MiB of HBM per device.

v0:
```python
import jax
import jax.numpy as jnp
from jax import lax
from jax.sharding import PartitionSpec as P

DECAY_RATE = 0.999
EPSILON = 1e-06
PRECISE = lax.Precision.HIGHEST


def body(grads, assign, left_factor, right_factor, left_root, right_root):
    fsdp_size = lax.axis_size("fsdp")
    dp_size = lax.axis_size("dp")
    blocks = grads.shape[1]
    shard_rows = grads.shape[2]
    width = grads.shape[3]
    col_width = width // dp_size
    member_id = lax.axis_index("dp")
    owners = jnp.arange(fsdp_size, dtype=jnp.int32)
    numbers = jnp.arange(blocks, dtype=jnp.int32)
    matches = (assign[:, None] == owners[None, :]).astype(jnp.int32)
    held = jnp.sum(numbers[:, None] * matches, axis=0)
    local_terms = grads[0].astype(jnp.float32)
    summed = lax.psum(local_terms, "dp")
    outgoing = jnp.take(summed, held, axis=0)
    arrived = lax.all_to_all(outgoing, "fsdp", split_axis=0, concat_axis=0, tiled=True)
    gathered = arrived.reshape(fsdp_size * shard_rows, width)
    own_cols = lax.dynamic_slice_in_dim(gathered, member_id * col_width, col_width, 1)
    contract_cols = (((1,), (1,)), ((), ()))
    contract_rows = (((0,), (0,)), ((), ()))
    own_rows = lax.dynamic_slice_in_dim(gathered, member_id * col_width, col_width, 0)
    left_out = DECAY_RATE * left_factor[0] + (1.0 - DECAY_RATE) * lax.dot_general(
        own_rows, gathered, contract_cols, precision=PRECISE
    )
    right_out = DECAY_RATE * right_factor[0] + (1.0 - DECAY_RATE) * lax.dot_general(
        own_cols, gathered, contract_rows, precision=PRECISE
    )
    sectioned = jnp.dot(left_root[0].astype(jnp.float32), gathered, precision=PRECISE)
    root_cols = right_root[0].astype(jnp.float32)
    conditioned = lax.dot_general(
        lax.all_gather(sectioned, "dp", axis=0, tiled=True),
        root_cols,
        contract_cols,
        precision=PRECISE,
    )
    block_square = jnp.sum(gathered * gathered)
    shaped_square = lax.psum(jnp.sum(conditioned * conditioned), "dp")
    graft = jnp.sqrt((block_square + EPSILON) / (shaped_square + EPSILON))
    rounded = (conditioned * graft).astype(jnp.bfloat16).reshape(fsdp_size, shard_rows, col_width)
    returned = lax.all_to_all(rounded, "fsdp", split_axis=0, concat_axis=0, tiled=True)
    update = jnp.take(returned, assign, axis=0)
    return (update, left_out[None], right_out[None])


def solution(mesh):
    placed = (
        P("dp", None, "fsdp", None),
        P(),
        P("fsdp", "dp", None),
        P("fsdp", "dp", None),
        P("fsdp", "dp", None),
        P("fsdp", "dp", None),
    )
    return jax.shard_map(
        body,
        mesh=mesh,
        in_specs=placed,
        out_specs=(P(None, "fsdp", "dp"), P("fsdp", "dp", None), P("fsdp", "dp", None)),
        check_vma=False,
    )
```

profile of v0, /device:TPU:1, one launch (start us, length us, event | category | flops | bytes accessed | tf_op | source)
XLA Modules:
  0.0 368.4 jit_solution(14728635751461767721)
XLA Ops:
  7.2 0.0 copy-start
  7.2 0.0 all-reduce.2.cloned.1.call-start
  7.2 4.1 %bitcast_convert_fusion = f32[64,16,1024]{2,1,0:T(8,128)} fusion(bf16[1,64,16,1024]{3,2,1,0:T(8,128)(2,1)} %param.6), kind=kLoop, calls=%fused_computation.3 | loop fusion | flops 1048576 | bytes 6291456 | tf_op jit(solution)/shard_map/convert_element_type | solution.py:23
  11.3 0.0 all-reduce.2.cloned.1.call-update
  11.4 0.0 all-gather.2.cloned.1.call-start
  11.4 0.1 select_reduce_fusion
  11.5 120.8 %all-reduce.2.cloned.1.call-done = f32[64,16,1024]{2,1,0:T(8,128)} async-done(((f32[64,16,1024]{2,1,0:T(8,128)}), f32[64,16,1024]{2,1,0:T(8,128)}) %all-reduce.2.cloned.1.call-update) | async-done | bytes 4194320 | tf_op jit(solution)/shard_map/psum | solution.py:24
  132.3 5.0 %gather_fusion = f32[64,16,1024]{2,1,0:T(8,128)} fusion(f32[64,16,1024]{2,1,0:T(8,128)} %all-reduce.2.cloned.1.call-done, s32[1024]{0:T(1024)S(1)} %pad_clamp_fusion.1), kind=kCustom, calls=%fused_computation | custom fusion | bytes 8388864 | tf_op jit(solution)/shard_map/jit(_take)/gather | solution.py:25
  137.3 2.5 broadcast_select_fusion
  139.8 104.9 %all_to_all.10 = f32[64,16,1024]{2,1,0:T(8,128)S(1)} all-to-all(f32[64,16,1024]{2,1,0:T(8,128)S(1)} %broadcast_select_fusion), channel_id=1, replica_groups=mesh['fsdp'=64,'dp'=8] {'fsdp'}, dimensions={0} | all-to-all | bytes 8388608 | tf_op jit(solution)/shard_map/all_to_all | solution.py:26
  244.8 1.9 copy-done.1
  246.7 4.3 %convolution_bitcast_fusion = f32[128,1024]{0,1:T(8,128)} fusion(f32[1024,1024]{1,0:T(8,128)S(1)} %bitcast.31, bf16[1,128,1024]{2,1,0:T(8,128)(2,1)S(1)} %copy-done.5), kind=kOutput, calls=%fused_computation.7 | convolution fusion | flops 1610612736 | bytes 4980736 | tf_op jit(solution)/shard_map/dot_general | solution.py:38
  251.0 0.0 all-gather.2.cloned.1.call-update
  251.1 3.9 %multiply_reduce_fusion = f32[]{:T(128)} fusion(f32[64,16,1024]{2,1,0:T(8,128)} %copy-done.1), kind=kLoop, calls=%fused_computation.2 | loop fusion | flops 2097151 | bytes 4194308 | tf_op jit(solution)/shard_map/reduce_sum | solution.py:46
  255.6 53.7 %all-gather.2.cloned.1.call-done = f32[1024,1024]{0,1:T(8,128)} async-done(((f32[128,1024]{0,1:T(8,128)}), f32[1024,1024]{0,1:T(8,128)}) %all-gather.2.cloned.1.call-update) | async-done | bytes 4194320 | tf_op jit(solution)/shard_map/all_gather | solution.py:41
  309.4 6.2 %multiply_reduce_fusion.1 = (f32[]{:T(128)}, f32[1024,128]{1,0:T(8,128)S(1)}) fusion(f32[1024,1024]{0,1:T(8,128)} %all-gather.2.cloned.1.call-done, bf16[1,128,1024]{2,1,0:T(8,128)(2,1)S(1)} %copy-done), kind=kOutput, calls=%fused_computation.15 | convolution fusion | flops 1610874880 | bytes 4980740 | tf_op jit(solution)/shard_map/dot_general | solution.py:40
  315.6 12.5 %psum.15 = f32[]{:T(128)} all-reduce(f32[]{:T(128)} %get-tuple-element.3), channel_id=1, replica_groups=mesh['fsdp'=64,'dp'=8] {'dp'}, use_global_device_ids=true, to_apply=%region_4.5 | all-reduce | flops 1 | bytes 8 | tf_op jit(solution)/shard_map/psum | solution.py:47
  328.8 0.7 multiply_convert_fusion
  329.6 17.3 %all-to-all-start.1 = ((bf16[64,16,128]{2,1,0:T(8,128)(2,1)}), bf16[64,16,128]{2,1,0:T(8,128)(2,1)S(1)}, u32[]{:S(2)}, u32[]{:S(2)}) async-start(bf16[64,16,128]{2,1,0:T(8,128)(2,1)} %bitcast.7), calls=%async_computation.1 | async-start | bytes 524288 | tf_op jit(solution)/shard_map/all_to_all | solution.py:50
  346.9 7.7 %fusion.1 = f32[1,128,1024]{2,1,0:T(8,128)} fusion(f32[1024,1024]{1,0:T(8,128)} %bitcast.32, s32[]{:T(128)S(6)} %select_n.37, f32[1,128,1024]{2,1,0:T(8,128)S(1)} %copy-done.3), kind=kOutput, calls=%fused_computation.9 | convolution fusion | flops 1611005952 | bytes 5767172 | tf_op jit(solution)/shard_map/dot_general | solution.py:32
  354.6 3.3 fusion.3
  357.9 2.1 all-to-all-done.1
  360.1 0.6 gather_fusion.1
  360.7 0.8 broadcast_select_fusion.1
  (18 shorter events, 0.1 us)
Async XLA Ops:
  7.2 302.2 %copy-start = (bf16[1,128,1024]{2,1,0:T(8,128)(2,1)S(1)}, bf16[1,128,1024]{2,1,0:T(8,128)(2,1)}, u32[]{:S(2)}) copy-start(bf16[1,128,1024]{2,1,0:T(8,128)(2,1)} %param.11) | copy-start | bytes 786436
  7.2 4.2 %copy-start.6 = (s32[64]{0:T(128)S(1)}, s32[64]{0:T(128)}, u32[]{:S(2)}) copy-start(s32[64]{0:T(128)} %param.7) | copy-start | bytes 772
  7.2 125.1 %all-reduce.2.cloned.1.call-start = ((), (), s32[]{:S(2)}) async-start(), calls=%async_computation.2 | async-start | bytes 8388608 | tf_op jit(solution)/shard_map/psum | solution.py:24
  11.4 298.0 %all-gather.2.cloned.1.call-start = ((), (), s32[]{:S(2)}) async-start(), calls=%async_computation.3 | async-start | bytes 4718592 | tf_op jit(solution)/shard_map/all_gather | solution.py:41
  139.8 106.9 %copy-start.5 = (bf16[1,128,1024]{2,1,0:T(8,128)(2,1)S(1)}, bf16[1,128,1024]{2,1,0:T(8,128)(2,1)}, u32[]{:S(2)}) copy-start(bf16[1,128,1024]{2,1,0:T(8,128)(2,1)} %param.10) | copy-start | bytes 786436
  244.8 1.9 copy-start.1
  254.9 92.0 %copy-start.3 = (f32[1,128,1024]{2,1,0:T(8,128)S(1)}, f32[1,128,1024]{2,1,0:T(8,128)}, u32[]{:S(2)}) copy-start(f32[1,128,1024]{2,1,0:T(8,128)} %param.8) | copy-start | bytes 1572868
  315.6 39.1 %copy-start.4 = (f32[1,128,1024]{2,1,0:T(8,128)S(1)}, f32[1,128,1024]{2,1,0:T(8,128)}, u32[]{:S(2)}) copy-start(f32[1,128,1024]{2,1,0:T(8,128)} %param.9) | copy-start | bytes 1572868
  329.6 30.5 %all-to-all-start.1 = ((bf16[64,16,128]{2,1,0:T(8,128)(2,1)}), bf16[64,16,128]{2,1,0:T(8,128)(2,1)S(1)}, u32[]{:S(2)}, u32[]{:S(2)}) async-start(bf16[64,16,128]{2,1,0:T(8,128)(2,1)} %bitcast.7), calls=%async_computation.1 | async-start | bytes 524288 | tf_op jit(solution)/shard_map/all_to_all | solution.py:50
  346.9 7.7 %copy-start.2 = (f32[64,16,1024]{2,1,0:T(8,128)S(1)}, f32[64,16,1024]{2,1,0:T(8,128)}, u32[]{:S(2)}) copy-start(f32[64,16,1024]{2,1,0:T(8,128)} %copy-done.1) | copy-start | bytes 12582916
Sparse Core Ops, SparseCore 0:
  11.5 120.8 all-reduce.1
  251.1 58.1 all-gather.1
where the time goes:
time: 369 us; the launch traced here: 368 us
  waiting for transfers between devices  177 us (48%)
  blocking collectives  117 us (32%)
  matrix products  21.5 us (6%)
  starting transfers between devices  17.4 us (5%)
  between operations  15.6 us (4%)
  other arithmetic  12.2 us (3%)
  local copies, waits for them, and re-layouts  7.56 us (2%)
    psum x1, waiting for transfers between devices, body(): summed = lax.psum(local_terms, 'dp')  121 us
    all_to_all x1, blocking collectives, body(): lax.all_to_all(outgoing, 'fsdp', split_axis=0, concat_axis=0, tiled=True)  105 us
    all_gather x1, waiting for transfers between devices, body(): lax.all_gather(sectioned, 'dp', axis=0, tiled=True)  53.7 us
    all_to_all x1, starting transfers between devices, body(): lax.all_to_all(rounded, 'fsdp', split_axis=0, concat_axis=0, tiled=True)  17.3 us
    psum x1, blocking collectives, body(): shaped_square = lax.psum(jnp.sum(conditioned * conditioned), 'dp')  12.5 us
    dot_general x1, matrix products, body(): lax.dot_general(own_rows, gathered, contract_cols, precision=PRECISE)  7.7 us
  transfers between devices with their start and end apart: 3, of which 3 were waited for; matrix products, arithmetic and copies ran while one was open for 4% of the time, Pallas kernels for 0%

commit v1 on v0

v1 whole, which is shorter than its diff:
```python
import jax
import jax.numpy as jnp
from jax import lax
from jax.sharding import PartitionSpec as P

DECAY_RATE = 0.999
EPSILON = 1e-06
PRECISE = lax.Precision.HIGHEST
STEPS = 128.0
TOP = 32767.0
FLOOR = 1e-30


def code_of(peak):
    return jnp.ceil(jnp.log2(jnp.maximum(peak, FLOOR)) * STEPS)


def scale_of(code):
    return jnp.exp2(code * (1.0 / STEPS)) * (1.0 / TOP)


def body(grads, assign, left_factor, right_factor, left_root, right_root):
    fsdp_size = lax.axis_size("fsdp")
    dp_size = lax.axis_size("dp")
    blocks = grads.shape[1]
    shard_rows = grads.shape[2]
    width = grads.shape[3]
    col_width = width // dp_size
    member_id = lax.axis_index("dp")
    owners = jnp.arange(fsdp_size, dtype=jnp.int32)
    numbers = jnp.arange(blocks, dtype=jnp.int32)
    matches = (assign[:, None] == owners[None, :]).astype(jnp.int32)
    held = jnp.sum(numbers[:, None] * matches, axis=0)
    left_full = lax.all_gather(left_root[0], "dp", axis=0, tiled=True)
    outgoing = jnp.take(grads[0], held, axis=0, mode="clip")
    outgoing = outgoing.reshape(fsdp_size, shard_rows, dp_size, col_width).transpose(0, 2, 1, 3)
    outgoing = outgoing.reshape(fsdp_size * dp_size, shard_rows, col_width)
    arrived = lax.all_to_all(outgoing, ("fsdp", "dp"), split_axis=0, concat_axis=0, tiled=True)
    terms = arrived.reshape(fsdp_size, dp_size, shard_rows, col_width).astype(jnp.float32)
    own = jnp.sum(terms, axis=1).reshape(width, col_width)
    codes = code_of(jnp.max(jnp.abs(own), axis=1))
    units = jnp.clip(jnp.round(own / scale_of(codes)[:, None]), -TOP, TOP).astype(jnp.int16)
    packed = jnp.concatenate([units, codes.astype(jnp.int16).reshape(-1, col_width)], axis=0)
    spread = lax.all_gather(packed, "dp", axis=0)
    scales = scale_of(spread[:, width:].reshape(dp_size, width).astype(jnp.float32))
    slabs = spread[:, :width].astype(jnp.float32) * scales[:, :, None]
    gathered = slabs.transpose(1, 0, 2).reshape(width, width)
    contract_cols = (((1,), (1,)), ((), ()))
    contract_rows = (((0,), (0,)), ((), ()))
    own_rows = lax.dynamic_slice_in_dim(gathered, member_id * col_width, col_width, 0)
    own_cols = lax.dynamic_slice_in_dim(gathered, member_id * col_width, col_width, 1)
    right_cols = lax.dot_general(
        gathered, right_root[0].astype(jnp.float32), contract_cols, precision=PRECISE
    )
    conditioned = jnp.dot(left_full.astype(jnp.float32), right_cols, precision=PRECISE)
    block_square = jnp.sum(gathered * gathered)
    shaped_square = lax.psum(jnp.sum(conditioned * conditioned), "dp")
    graft = jnp.sqrt((block_square + EPSILON) / (shaped_square + EPSILON))
    rounded = (conditioned * graft).astype(jnp.bfloat16).reshape(fsdp_size, shard_rows, col_width)
    returned = lax.all_to_all(rounded, "fsdp", split_axis=0, concat_axis=0, tiled=True)
    left_out = DECAY_RATE * left_factor[0] + (1.0 - DECAY_RATE) * lax.dot_general(
        own_rows, gathered, contract_cols, precision=PRECISE
    )
    right_out = DECAY_RATE * right_factor[0] + (1.0 - DECAY_RATE) * lax.dot_general(
        own_cols, gathered, contract_rows, precision=PRECISE
    )
    update = jnp.take(returned, assign, axis=0, mode="clip")
    return (update, left_out[None], right_out[None])


def solution(mesh):
    placed = (
        P("dp", None, "fsdp", None),
        P(),
        P("fsdp", "dp", None),
        P("fsdp", "dp", None),
        P("fsdp", "dp", None),
        P("fsdp", "dp", None),
    )
    return jax.shard_map(
        body,
        mesh=mesh,
        in_specs=placed,
        out_specs=(P(None, "fsdp", "dp"), P("fsdp", "dp", None), P("fsdp", "dp", None)),
        check_vma=False,
    )
```

time: 369 us -> 204 us (0.55)
  waiting for transfers between devices: 177 us -> 54.1 us
  blocking collectives: 117 us -> 45.4 us
  starting transfers between devices: 17.4 us -> 40.8 us
  local copies, waits for them, and re-layouts: 7.56 us -> 16.2 us
    psum x1 -> x0, waiting for transfers between devices: 121 us -> none  [body(): summed = lax.psum(local_terms, 'dp')]
    all_to_all x1 -> x0, blocking collectives: 105 us -> none  [body(): lax.all_to_all(outgoing, 'fsdp', split_axis=0, concat_axis=0, tiled=True)]
    all_gather x1, waiting for transfers between devices: 53.7 us -> 0.02 us  [body(): left_full = lax.all_gather(left_root[0], 'dp', axis=0, tiled=True)]
    all_to_all x0 -> x1, waiting for transfers between devices: none -> 51.4 us  [body(): lax.all_to_all(outgoing, ('fsdp', 'dp'), split_axis=0, concat_axis=0, til...]
    all_gather x0 -> x1, blocking collectives: none -> 32.8 us  [body(): spread = lax.all_gather(packed, 'dp', axis=0)]
    all_to_all x0 -> x1, starting transfers between devices: none -> 24.2 us  [body(): lax.all_to_all(outgoing, ('fsdp', 'dp'), split_axis=0, concat_axis=0, til...]
    transpose x0 -> x3, local copies, waits for them, and re-layouts: none -> 7.53 us  [the longest x1 5.35 us: body(): gathered = slabs.transpose(1, 0, 2).reshape(width, width)]
    convert_element_type x1, other arithmetic: 4.09 us -> 0.21 us  [body(): jnp.clip(jnp.round(own / scale_of(codes)[:, None]), -TOP, TOP)]
  transfers between devices with their start and end apart: 3 -> 3, of which waited for: 3 -> 2; matrix products, arithmetic and copies ran while one was open for 4% -> 16% of each run, Pallas kernels for 0% -> 0%
where the time goes in v1:
time: 204 us; the launch traced here: 203 us
  waiting for transfers between devices  54.1 us (27%)
  blocking collectives  45.4 us (22%)
  starting transfers between devices  40.8 us (20%)
  matrix products  20.7 us (10%)
  local copies, waits for them, and re-layouts  16.2 us (8%)
  between operations  15.6 us (8%)
  other arithmetic  10.4 us (5%)
    all_to_all x1, waiting for transfers between devices, body(): lax.all_to_all(outgoing, ('fsdp', 'dp'), split_axis=0, concat_axis=0, til...  51.4 us
    all_gather x1, blocking collectives, body(): spread = lax.all_gather(packed, 'dp', axis=0)  32.8 us
    all_to_all x1, starting transfers between devices, body(): lax.all_to_all(outgoing, ('fsdp', 'dp'), split_axis=0, concat_axis=0, til...  24.2 us
    all_to_all x1, starting transfers between devices, body(): lax.all_to_all(rounded, 'fsdp', split_axis=0, concat_axis=0, tiled=True)  16.6 us
    psum x1, blocking collectives, body(): shaped_square = lax.psum(jnp.sum(conditioned * conditioned), 'dp')  12.6 us
    dot_general x1, matrix products, body(): lax.dot_general(own_rows, gathered, contract_cols, precision=PRECISE)  5.83 us
    dot_general x1, matrix products, body(): lax.dot_general(gathered, right_root[0].astype(jnp.float32), contract_col...  5.63 us
    transpose x1, local copies, waits for them, and re-layouts, body(): gathered = slabs.transpose(1, 0, 2).reshape(width, width)  5.35 us
  transfers between devices with their start and end apart: 3, of which 2 were waited for; matrix products, arithmetic and copies ran while one was open for 16% of the time, Pallas kernels for 0%

profile of v1, /device:TPU:1, one launch (start us, length us, event | category | flops | bytes accessed | tf_op | source)
XLA Modules:
  0.0 203.2 jit_solution(15946960378836424131)
XLA Ops:
  7.2 0.9 select_reduce_fusion
  8.1 0.7 copy-done
  8.8 2.0 gather_fusion
  10.8 2.2 %copy.16 = bf16[128,8,8,128]{3,2,1,0:T(8,128)(2,1)S(1)} copy(bf16[128,8,8,128]{3,1,2,0:T(8,128)(2,1)} %bitcast.63) | data formatting | bytes 4194304
  13.0 0.2 bitcast_bitcast_fusion
  13.3 1.9 copy.13
  15.2 24.2 %all-to-all-start = ((bf16[512,16,128]{2,1,0:T(8,128)(2,1)}), bf16[512,16,128]{2,1,0:T(8,128)(2,1)}, u32[]{:S(2)}, u32[]{:S(2)}) async-start(bf16[512,16,128]{2,1,0:T(8,128)(2,1)} %bitcast.62), calls=%async_computation | async-start | bytes 4194304 | tf_op jit(solution)/shard_map/all_to_all | solution.py:38
  39.5 0.7 all-gather.5.cloned.1.call-update
  40.2 51.4 %all-to-all-done = bf16[512,16,128]{2,1,0:T(8,128)(2,1)} async-done(((bf16[512,16,128]{2,1,0:T(8,128)(2,1)}), bf16[512,16,128]{2,1,0:T(8,128)(2,1)}, u32[]{:S(2)}, u32[]{:S(2)}) %all-to-all-start) | async-done | bytes 2097184 | tf_op jit(solution)/shard_map/all_to_all | solution.py:38
  91.6 2.1 %convert_reduce_fusion = f32[64,16,128]{2,1,0:T(8,128)S(1)} fusion(bf16[512,16,128]{2,1,0:T(8,128)(2,1)} %all-to-all-done), kind=kLoop, calls=%fused_computation.2 | loop fusion | flops 1966080 | bytes 2621440 | tf_op jit(solution)/shard_map/reduce_sum | solution.py:40
  94.4 32.8 %all-gather.6 = s16[8256,128]{1,0:T(8,128)(2,1)S(1)} all-gather(s16[1032,128]{1,0:T(8,128)(2,1)S(1)} %pad_add_fusion), channel_id=2, replica_groups=mesh['fsdp'=64,'dp'=8] {'dp'}, dimensions={0}, use_global_device_ids=true | all-gather | bytes 2377728 | tf_op jit(solution)/shard_map/all_gather | solution.py:44
  127.3 1.4 copy-done.2
  128.6 3.1 %multiply_bitcast_fusion = f32[1024,8,128]{2,0,1:T(8,128)} fusion(s16[8,1032,128]{2,1,0:T(8,128)(2,1)S(1)} %bitcast.60, f32[8,1024]{1,0:T(8,128)S(1)} %bitcast.65), kind=kLoop, calls=%fused_computation.4 | loop fusion | flops 2097152 | bytes 6324224 | tf_op jit(solution)/shard_map/transpose | solution.py:47
  131.7 5.3 %copy.14 = f32[1024,8,128]{0,2,1:T(8,128)} copy(f32[1024,8,128]{2,0,1:T(8,128)} %multiply_bitcast_fusion) | data formatting | bytes 8388608 | tf_op jit(solution)/shard_map/transpose | solution.py:47
  137.0 3.8 %multiply_reduce_fusion = f32[]{:T(128)} fusion(f32[8,1024]{1,0:T(8,128)S(1)} %bitcast.66, s16[8,1032,128]{2,1,0:T(8,128)(2,1)} %bitcast.61), kind=kLoop, calls=%fused_computation.3 | loop fusion | flops 4194303 | bytes 2129924 | tf_op jit(solution)/shard_map/reduce_sum | solution.py:56
  140.8 5.6 %fusion.12 = f32[1024,128]{1,0:T(8,128)S(1)} fusion(f32[1024,1024]{0,1:T(8,128)} %bitcast.56, bf16[1,128,1024]{2,1,0:T(8,128)(2,1)S(1)} %copy-done.4), kind=kOutput, calls=%fused_computation.25 | convolution fusion | flops 1610612736 | bytes 4980736 | tf_op jit(solution)/shard_map/dot_general | solution.py:52
  146.4 4.0 %multiply_reduce_fusion.1 = (f32[]{:T(128)}, f32[128,1024]{1,0:T(8,128)S(1)}) fusion(f32[1024,128]{1,0:T(8,128)S(1)} %fusion.12, bf16[1,1024,1024]{2,1,0:T(8,128)(2,1)} %all-gather.5.cloned.1.call-done), kind=kOutput, calls=%fused_computation.21 | convolution fusion | flops 1610874880 | bytes 3145732 | tf_op jit(solution)/shard_map/dot_general | solution.py:55
  150.4 12.6 %psum.7 = f32[]{:T(128)} all-reduce(f32[]{:T(128)} %get-tuple-element.5), channel_id=1, replica_groups=mesh['fsdp'=64,'dp'=8] {'dp'}, use_global_device_ids=true, to_apply=%region_5.6 | all-reduce | flops 1 | bytes 8 | tf_op jit(solution)/shard_map/psum | solution.py:57
  164.5 0.8 copy.15
  165.3 16.6 %all-to-all-start.1 = ((bf16[64,16,128]{2,1,0:T(8,128)(2,1)}), bf16[64,16,128]{2,1,0:T(8,128)(2,1)S(1)}, u32[]{:S(2)}, u32[]{:S(2)}) async-start(bf16[64,16,128]{2,1,0:T(8,128)(2,1)} %bitcast.11), calls=%async_computation.1 | async-start | bytes 524288 | tf_op jit(solution)/shard_map/all_to_all | solution.py:60
  181.9 5.8 %fusion.3 = f32[1,128,1024]{2,1,0:T(8,128)} fusion(f32[1024,1024]{0,1:T(8,128)} %bitcast.57, s32[]{:T(128)S(6)} %select_n.4, f32[1,128,1024]{2,1,0:T(8,128)} %param.8), kind=kOutput, calls=%fused_computation.11 | convolution fusion | flops 1611005952 | bytes 5767172 | tf_op jit(solution)/shard_map/dot_general | solution.py:61
  187.8 5.3 %fusion.5 = f32[1,128,1024]{2,1,0:T(8,128)} fusion(f32[1024,1024]{0,1:T(8,128)S(1)} %bitcast.58, s32[]{:T(128)S(6)} %select_n.4, f32[1,128,1024]{2,1,0:T(8,128)S(1)} %copy-done.3), kind=kOutput, calls=%fused_computation.13 | convolution fusion | flops 1611005952 | bytes 5767172 | tf_op jit(solution)/shard_map/dot_general | solution.py:64
  193.0 2.0 %all-to-all-done.1 = bf16[64,16,128]{2,1,0:T(8,128)(2,1)S(1)} async-done(((bf16[64,16,128]{2,1,0:T(8,128)(2,1)}), bf16[64,16,128]{2,1,0:T(8,128)(2,1)S(1)}, u32[]{:S(2)}, u32[]{:S(2)}) %all-to-all-start.1) | async-done | bytes 262176 | tf_op jit(solution)/shard_map/all_to_all | solution.py:60
  195.1 1.3 gather_fusion.1
  (23 shorter events, 0.8 us)
Async XLA Ops:
  7.2 1.6 copy-start
  15.2 25.0 %copy-start.5 = (s32[64]{0:T(128)S(1)}, s32[64]{0:T(128)}, u32[]{:S(2)}) copy-start(s32[64]{0:T(128)} %param.7) | copy-start | bytes 772
  15.2 76.4 %all-to-all-start = ((bf16[512,16,128]{2,1,0:T(8,128)(2,1)}), bf16[512,16,128]{2,1,0:T(8,128)(2,1)}, u32[]{:S(2)}, u32[]{:S(2)}) async-start(bf16[512,16,128]{2,1,0:T(8,128)(2,1)} %bitcast.62), calls=%async_computation | async-start | bytes 4194304 | tf_op jit(solution)/shard_map/all_to_all | solution.py:38
  39.5 107.0 %all-gather.5.cloned.1.call-start = ((), (), s32[]{:S(2)}) async-start(), calls=%async_computation.2 | async-start | bytes 2359296 | tf_op jit(solution)/shard_map/all_gather | solution.py:34
  127.2 1.4 copy-start.2
  137.0 3.8 %copy-start.4 = (bf16[1,128,1024]{2,1,0:T(8,128)(2,1)S(1)}, bf16[1,128,1024]{2,1,0:T(8,128)(2,1)}, u32[]{:S(2)}) copy-start(bf16[1,128,1024]{2,1,0:T(8,128)(2,1)} %param.11) | copy-start | bytes 786436
  165.3 29.7 %all-to-all-start.1 = ((bf16[64,16,128]{2,1,0:T(8,128)(2,1)}), bf16[64,16,128]{2,1,0:T(8,128)(2,1)S(1)}, u32[]{:S(2)}, u32[]{:S(2)}) async-start(bf16[64,16,128]{2,1,0:T(8,128)(2,1)} %bitcast.11), calls=%async_computation.1 | async-start | bytes 524288 | tf_op jit(solution)/shard_map/all_to_all | solution.py:60
  181.9 5.9 %copy-start.1 = (f32[1024,8,128]{0,2,1:T(8,128)S(1)}, f32[1024,8,128]{0,2,1:T(8,128)}, u32[]{:S(2)}) copy-start(f32[1024,8,128]{0,2,1:T(8,128)} %copy.14) | copy-start | bytes 12582916
  181.9 5.9 %copy-start.3 = (f32[1,128,1024]{2,1,0:T(8,128)S(1)}, f32[1,128,1024]{2,1,0:T(8,128)}, u32[]{:S(2)}) copy-start(f32[1,128,1024]{2,1,0:T(8,128)} %param.9) | copy-start | bytes 1572868
Sparse Core Ops, SparseCore 0:
  42.4 73.4 all-gather.4

commit v2 on v1

v2 whole, which is shorter than its diff:
```python
import functools

import jax
import jax.numpy as jnp
from jax import lax
from jax.experimental import pallas as pl
from jax.experimental.pallas import tpu as pltpu
from jax.sharding import PartitionSpec as P

DECAY_RATE = 0.999
EPSILON = 1e-06
STEPS = 90.0
TOP = 32767.0
FLOOR = 1e-30
CODES = 16
MIB = 1 << 20


def vmem():
    return pl.BlockSpec(memory_space=pltpu.VMEM)


def anywhere():
    return pl.BlockSpec(memory_space=pl.ANY)


def cost(flops, moved):
    return pl.CostEstimate(flops=flops, bytes_accessed=moved, transcendentals=0)


def send_kernel(dp_size, assign_ref, grads_ref, out_ref, held, turned, in_sems, out_sem):
    blocks = grads_ref.shape[0]
    col_width = grads_ref.shape[2] // dp_size
    chunks = in_sems.shape[0]
    chunk = blocks // chunks
    loads = [
        pltpu.make_async_copy(
            grads_ref.at[pl.ds(c * chunk, chunk)], held.at[pl.ds(c * chunk, chunk)], in_sems.at[c]
        )
        for c in range(chunks)
    ]
    for load in loads:
        load.start()
    for c in range(chunks):
        loads[c].wait()

        def turn(b, carry):
            for k in range(dp_size):
                turned[b, k] = held[b, :, pl.ds(k * col_width, col_width)]
            pltpu.make_async_copy(turned.at[b], out_ref.at[assign_ref[b]], out_sem).start()
            return carry

        lax.fori_loop(c * chunk, (c + 1) * chunk, turn, 0)
    pltpu.make_async_copy(turned, out_ref, out_sem).wait()


def send(assign, grads, dp_size):
    blocks, rows, width = grads.shape
    shape = (blocks, dp_size, rows, width // dp_size)
    return pl.pallas_call(
        functools.partial(send_kernel, dp_size),
        out_shape=jax.ShapeDtypeStruct(shape, grads.dtype),
        in_specs=[pl.BlockSpec(memory_space=pltpu.SMEM), anywhere()],
        out_specs=anywhere(),
        scratch_shapes=[
            pltpu.VMEM(grads.shape, grads.dtype),
            pltpu.VMEM(shape, grads.dtype),
            pltpu.SemaphoreType.DMA((4,)),
            pltpu.SemaphoreType.DMA,
        ],
        compiler_params=pltpu.CompilerParams(vmem_limit_bytes=16 * MIB),
        cost_estimate=cost(0, 2 * grads.size * 2),
        name="send",
    )(assign, grads)


def scale_of(code):
    return jnp.exp(code * (1.0 / STEPS)) * (1.0 / TOP)


def fold_kernel(arrived_ref, packed_ref):
    shards, replicas, rows, width = arrived_ref.shape
    group = shards // CODES
    codes = []
    for g in range(CODES):
        terms = arrived_ref[pl.ds(g * group, group)].astype(jnp.float32)
        total = jnp.sum(terms, axis=1).reshape(group * rows, width)
        peak = jnp.maximum(jnp.max(jnp.abs(total), axis=0, keepdims=True), FLOOR)
        code = jnp.ceil(jnp.log(peak) * STEPS)
        units = jnp.floor(total * (1.0 / scale_of(code)) + 0.5)
        units = jnp.clip(units, -TOP, TOP).astype(jnp.int32).astype(jnp.int16)
        packed_ref[pl.ds(g * group * rows, group * rows), :] = units
        codes.append(code)
    codes = jnp.concatenate(codes, axis=0).astype(jnp.int32).astype(jnp.int16)
    packed_ref[pl.ds(shards * rows, CODES), :] = codes


def fold(arrived):
    shards, replicas, rows, width = arrived.shape
    return pl.pallas_call(
        fold_kernel,
        out_shape=jax.ShapeDtypeStruct((shards * rows + CODES, width), jnp.int16),
        in_specs=[vmem()],
        out_specs=vmem(),
        compiler_params=pltpu.CompilerParams(vmem_limit_bytes=16 * MIB),
        cost_estimate=cost(arrived.size, 2 * arrived.size),
        name="fold",
    )(arrived)


def unpack(spread_ref, k, high, low):
    width = spread_ref.shape[2]
    size = spread_ref.shape[1] - CODES
    rows = size // CODES
    columns = pl.ds(k * width, width)
    scales = scale_of(spread_ref[k, pl.ds(size, CODES), :].astype(jnp.int32).astype(jnp.float32))
    square = jnp.zeros((8, width), jnp.float32)
    for g in range(CODES):
        here = pl.ds(g * rows, rows)
        units = spread_ref[k, here, :].astype(jnp.int32).astype(jnp.float32)
        values = units * scales[g : g + 1]
        upper = values.astype(jnp.bfloat16)
        high[here, columns] = upper
        low[here, columns] = (values - upper.astype(jnp.float32)).astype(jnp.bfloat16)
        square = square + jnp.sum((values * values).reshape(rows // 8, 8, width), axis=0)
    return square


NT = (((1,), (1,)), ((), ()))
NN = (((1,), (0,)), ((), ()))


def dot(a, b, dims):
    return lax.dot_general(a, b, dims, preferred_element_type=jnp.float32)


def shape_kernel(spread_ref, left_ref, right_ref, out_ref, squares_ref, total_ref, high, low, mid):
    slabs = spread_ref.shape[0]
    size, width = out_ref.shape
    tile = 256
    square = jnp.zeros((8, width), jnp.float32)
    for k in range(slabs):
        square = square + unpack(spread_ref, k, high, low)
    total_ref[...] = square

    def right_step(t, carry):
        rows = pl.ds(pl.multiple_of(t * tile, tile), tile)
        part = dot(high[rows, :], right_ref[...], NT) + dot(low[rows, :], right_ref[...], NT)
        upper = part.astype(jnp.bfloat16)
        mid[rows, pl.ds(0, width)] = upper
        mid[rows, pl.ds(width, width)] = (part - upper.astype(jnp.float32)).astype(jnp.bfloat16)
        return carry

    lax.fori_loop(0, size // tile, right_step, 0)

    def left_step(t, square):
        rows = pl.ds(pl.multiple_of(t * tile, tile), tile)
        both = dot(left_ref[rows, :], mid[...], NN)
        part = both[:, :width] + both[:, width:]
        out_ref[rows, :] = part
        return square + jnp.sum((part * part).reshape(tile // 8, 8, width), axis=0)

    square = lax.fori_loop(0, size // tile, left_step, jnp.zeros((8, width), jnp.float32))
    for k in range(slabs):
        squares_ref[k] = square


def shape(spread, left, right):
    slabs, _, width = spread.shape
    size = left.shape[0]
    return pl.pallas_call(
        shape_kernel,
        out_shape=(
            jax.ShapeDtypeStruct((size, width), jnp.float32),
            jax.ShapeDtypeStruct((slabs, 8, width), jnp.float32),
            jax.ShapeDtypeStruct((8, width), jnp.float32),
        ),
        in_specs=[vmem()] * 3,
        out_specs=(vmem(),) * 3,
        scratch_shapes=[
            pltpu.VMEM((size, size), jnp.bfloat16),
            pltpu.VMEM((size, size), jnp.bfloat16),
            pltpu.VMEM((size, 2 * width), jnp.bfloat16),
        ],
        compiler_params=pltpu.CompilerParams(vmem_limit_bytes=24 * MIB),
        cost_estimate=cost(8 * size * size * width, 6 * size * size),
        name="shape",
    )(spread, left, right)


def graft_kernel(shaped_ref, squares_ref, total_ref, out_ref):
    def whole(x):
        return jnp.sum(jnp.sum(x, axis=0, keepdims=True), axis=1, keepdims=True)

    shaped_square = whole(jnp.sum(squares_ref[...], axis=0))
    block_square = whole(total_ref[...])
    ratio = jnp.sqrt((block_square + EPSILON) / (shaped_square + EPSILON))
    out_ref[...] = (shaped_ref[...] * ratio).astype(jnp.bfloat16)


def graft(shaped, squares, total):
    return pl.pallas_call(
        graft_kernel,
        out_shape=jax.ShapeDtypeStruct(shaped.shape, jnp.bfloat16),
        in_specs=[vmem()] * 3,
        out_specs=vmem(),
        compiler_params=pltpu.CompilerParams(vmem_limit_bytes=8 * MIB),
        cost_estimate=cost(shaped.size, 6 * shaped.size),
        name="graft",
    )(shaped, squares, total)


def stats_kernel(place_ref, spread_ref, left_ref, right_ref, left_out, right_out, high, low, turned):
    slabs = spread_ref.shape[0]
    rows, size = left_ref.shape
    tile = 256
    for k in range(slabs):
        unpack(spread_ref, k, high, low)
    own = pl.ds(pl.multiple_of(place_ref[0] * rows, rows), rows)
    turned[pl.ds(0, rows), :] = high[:, own].T
    turned[pl.ds(rows, rows), :] = low[:, own].T

    def step(t, carry):
        here = pl.ds(pl.multiple_of(t * tile, tile), tile)
        part = dot(high[own, :], high[here, :], NT)
        part += dot(low[own, :], high[here, :], NT)
        part += dot(high[own, :], low[here, :], NT)
        left_out[:, here] = DECAY_RATE * left_ref[:, here] + (1.0 - DECAY_RATE) * part
        both = dot(turned[...], high[:, here], NN)
        part = both[:rows] + both[rows:] + dot(turned[pl.ds(0, rows), :], low[:, here], NN)
        right_out[:, here] = DECAY_RATE * right_ref[:, here] + (1.0 - DECAY_RATE) * part
        return carry

    lax.fori_loop(0, size // tile, step, 0)


def stats(place, spread, left, right):
    rows, size = left.shape
    return pl.pallas_call(
        stats_kernel,
        out_shape=(jax.ShapeDtypeStruct(left.shape, left.dtype),) * 2,
        in_specs=[pl.BlockSpec(memory_space=pltpu.SMEM)] + [vmem()] * 3,
        out_specs=(vmem(),) * 2,
        scratch_shapes=[
            pltpu.VMEM((size, size), jnp.bfloat16),
            pltpu.VMEM((size, size), jnp.bfloat16),
            pltpu.VMEM((2 * rows, size), jnp.bfloat16),
        ],
        compiler_params=pltpu.CompilerParams(vmem_limit_bytes=24 * MIB),
        cost_estimate=cost(12 * size * size * rows, 6 * size * size),
        name="stats",
    )(place, spread, left, right)


def body(grads, assign, left_factor, right_factor, left_root, right_root):
    fsdp_size = lax.axis_size("fsdp")
    dp_size = lax.axis_size("dp")
    shard_rows = grads.shape[2]
    width = grads.shape[3]
    col_width = width // dp_size
    place = lax.axis_index("dp").astype(jnp.int32).reshape(1)
    left_full = lax.all_gather(left_root[0], "dp", axis=0, tiled=True)
    outgoing = send(assign, grads[0], dp_size)
    outgoing = outgoing.reshape(fsdp_size * dp_size, shard_rows, col_width)
    arrived = lax.all_to_all(outgoing, ("fsdp", "dp"), split_axis=0, concat_axis=0, tiled=True)
    packed = fold(arrived.reshape(fsdp_size, dp_size, shard_rows, col_width))
    spread = lax.all_gather(packed, "dp", axis=0)
    shaped, squares, total = shape(spread, left_full, right_root[0])
    squares = lax.all_to_all(squares, "dp", split_axis=0, concat_axis=0, tiled=True)
    rounded = graft(shaped, squares, total).reshape(fsdp_size, shard_rows, col_width)
    rounded, spread = lax.optimization_barrier((rounded, spread))
    returned = lax.all_to_all(rounded, "fsdp", split_axis=0, concat_axis=0, tiled=True)
    left_out, right_out = stats(place, spread, left_factor[0], right_factor[0])
    update = jnp.take(returned, assign, axis=0, mode="clip")
    return (update, left_out[None], right_out[None])


def solution(mesh):
    placed = (
        P("dp", None, "fsdp", None),
        P(),
        P("fsdp", "dp", None),
        P("fsdp", "dp", None),
        P("fsdp", "dp", None),
        P("fsdp", "dp", None),
    )
    return jax.shard_map(
        body,
        mesh=mesh,
        in_specs=placed,
        out_specs=(P(None, "fsdp", "dp"), P("fsdp", "dp", None), P("fsdp", "dp", None)),
        check_vma=False,
    )
```

time: 204 us -> 179 us (0.88)
  matrix products: 20.7 us -> 0 us
  Pallas kernels: 0 us -> 16.1 us
  other arithmetic: 10.4 us -> 0.01 us
  local copies, waits for them, and re-layouts: 16.2 us -> 6.49 us
  waiting for transfers between devices: 54.1 us -> 61.2 us
  starting transfers between devices: 40.8 us -> 35.2 us
    dot_general x4 -> x0, matrix products: 20.7 us -> none  [the longest x1 5.83 us: body(): lax.dot_general(own_rows, gathered, contract_cols, precision=PRECISE)]
    pallas_call x0 -> x5, Pallas kernels: none -> 16.1 us  [the longest x1 6.03 us: stats(): pl.pallas_call(stats_kernel, out_shape=(jax.ShapeDtypeStruct(left.shape,...]
    psum x1 -> x0, blocking collectives: 12.6 us -> none  [body(): shaped_square = lax.psum(jnp.sum(conditioned * conditioned), 'dp')]
    all_to_all x0 -> x1, blocking collectives: none -> 9.82 us  [body(): lax.all_to_all(squares, 'dp', split_axis=0, concat_axis=0, tiled=True)]
    transpose x3 -> x0, local copies, waits for them, and re-layouts: 7.53 us -> none  [the longest x1 5.35 us: body(): gathered = slabs.transpose(1, 0, 2).reshape(width, width)]
    reduce_sum x3 -> x0, other arithmetic: 6.77 us -> none  [the longest x1 3.75 us: body(): block_square = jnp.sum(gathered * gathered)]
    all_to_all x1, waiting for transfers between devices: 2.04 us -> 7.09 us  [body(): lax.all_to_all(rounded, 'fsdp', split_axis=0, concat_axis=0, tiled=True)]
    all_to_all x1, starting transfers between devices: 16.6 us -> 13 us  [body(): lax.all_to_all(rounded, 'fsdp', split_axis=0, concat_axis=0, tiled=True)]
  transfers between devices with their start and end apart: 3 -> 3, of which waited for: 2 -> 2; matrix products, arithmetic and copies ran while one was open for 16% -> 0% of each run, Pallas kernels for 0% -> 4%
where the time goes in v2:
time: 179 us; the launch traced here: 178 us
  waiting for transfers between devices  61.2 us (34%)
  blocking collectives  45.1 us (25%)
  starting transfers between devices  35.2 us (20%)
  Pallas kernels  16.1 us (9%)
  between operations  14.1 us (8%)
  local copies, waits for them, and re-layouts  6.49 us (4%)
    all_to_all x1, waiting for transfers between devices, body(): lax.all_to_all(outgoing, ('fsdp', 'dp'), split_axis=0, concat_axis=0, til...  53.4 us
    all_gather x1, blocking collectives, body(): spread = lax.all_gather(packed, 'dp', axis=0)  35.3 us
    all_to_all x1, starting transfers between devices, body(): lax.all_to_all(outgoing, ('fsdp', 'dp'), split_axis=0, concat_axis=0, til...  22.2 us
    all_to_all x1, starting transfers between devices, body(): lax.all_to_all(rounded, 'fsdp', split_axis=0, concat_axis=0, tiled=True)  13 us
    all_to_all x1, blocking collectives, body(): lax.all_to_all(squares, 'dp', split_axis=0, concat_axis=0, tiled=True)  9.82 us
    all_to_all x1, waiting for transfers between devices, body(): lax.all_to_all(rounded, 'fsdp', split_axis=0, concat_axis=0, tiled=True)  7.09 us
    pallas_call x1, Pallas kernels, stats(): pl.pallas_call(stats_kernel, out_shape=(jax.ShapeDtypeStruct(left.shape,...  6.03 us
    unnamed x16, local copies, waits for them, and re-layouts  5.17 us
  transfers between devices with their start and end apart: 3, of which 2 were waited for; matrix products, arithmetic and copies ran while one was open for 0% of the time, Pallas kernels for 4%

profile of v2, /device:TPU:1, one launch (start us, length us, event | category | flops | bytes accessed | tf_op | source)
XLA Modules:
  0.0 178.2 jit_solution(35475830004118603)
XLA Ops:
  7.2 0.0 copy-start.1
  7.2 1.6 copy-done.1
  8.8 0.7 copy-done.4
  9.4 4.2 %send.1 = bf16[64,8,16,128]{3,2,1,0:T(8,128)(2,1)S(1)} custom-call(s32[64]{0:T(128)S(1)} %copy-done.4, bf16[64,16,1024]{2,1,0:T(8,128)(2,1)S(1)} %bitcast.16), custom_call_target="tpu_custom_call" | custom-call | bytes 4194304 | tf_op jit(solution)/shard_map/send/pallas_call | solution.py:60
  13.6 0.0 copy-start
  13.6 1.3 copy-done
  15.0 22.2 %all-to-all-start = ((bf16[512,16,128]{2,1,0:T(8,128)(2,1)}), bf16[512,16,128]{2,1,0:T(8,128)(2,1)S(1)}, u32[]{:S(2)}, u32[]{:S(2)}) async-start(bf16[512,16,128]{2,1,0:T(8,128)(2,1)} %bitcast.15), calls=%async_computation | async-start | bytes 4194304 | tf_op jit(solution)/shard_map/all_to_all | solution.py:265
  37.1 0.0 all-gather.5.cloned.1.call-start
  37.2 0.7 all-gather.5.cloned.1.call-update
  37.9 53.4 %all-to-all-done = bf16[512,16,128]{2,1,0:T(8,128)(2,1)S(1)} async-done(((bf16[512,16,128]{2,1,0:T(8,128)(2,1)}), bf16[512,16,128]{2,1,0:T(8,128)(2,1)S(1)}, u32[]{:S(2)}, u32[]{:S(2)}) %all-to-all-start) | async-done | bytes 2097184 | tf_op jit(solution)/shard_map/all_to_all | solution.py:265
  91.3 0.5 fold.1
  91.7 35.3 %all-gather.6 = s16[8320,128]{1,0:T(8,128)(2,1)S(1)} all-gather(s16[1040,128]{1,0:T(8,128)(2,1)S(1)} %fold.1), channel_id=2, replica_groups=mesh['fsdp'=64,'dp'=8] {'dp'}, dimensions={0}, use_global_device_ids=true | all-gather | bytes 2396160 | tf_op jit(solution)/shard_map/all_gather | solution.py:267
  127.0 0.0 copy-done.3
  127.0 1.6 copy-done.2
  128.6 4.5 %shape.1 = (f32[1024,128]{1,0:T(8,128)S(1)}, f32[8,8,128]{2,1,0:T(8,128)S(1)}, f32[8,128]{1,0:T(8,128)S(1)}) custom-call(s16[8,1040,128]{2,1,0:T(8,128)(2,1)S(1)} %bitcast.12, bf16[1024,1024]{1,0:T(8,128)(2,1)S(1)} %bitcast.17, bf16[128,1024]{1,0:T(8,128)(2,1)S(1)} %bitcast.18), custom_call_target="tpu_custom_call" | custom-call | flops 1073741824 | bytes 6291456 | tf_op jit(solution)/shard_map/shape/pallas_call | solution.py:171
  133.1 9.8 %all_to_all.15.squares_ref = f32[8,8,128]{2,1,0:T(8,128)S(1)} all-to-all(f32[8,8,128]{2,1,0:T(8,128)S(1)} %get-tuple-element.11), channel_id=1, replica_groups=mesh['fsdp'=64,'dp'=8] {'dp'}, dimensions={0} | all-to-all | bytes 65536 | tf_op jit(solution)/shard_map/all_to_all | solution.py:269
  143.0 0.9 graft.1
  143.8 13.0 %all-to-all-start.2 = ((bf16[64,16,128]{2,1,0:T(8,128)(2,1)}), bf16[64,16,128]{2,1,0:T(8,128)(2,1)S(1)}, u32[]{:S(2)}, u32[]{:S(2)}) async-start(bf16[64,16,128]{2,1,0:T(8,128)(2,1)} %bitcast.6), calls=%async_computation.2 | async-start | bytes 524288 | tf_op jit(solution)/shard_map/all_to_all | solution.py:272
  156.8 0.0 copy-done.5
  156.9 0.0 copy-done.6
  156.9 0.0 copy-done.7
  156.9 6.0 %stats.1 = (f32[128,1024]{1,0:T(8,128)}, f32[128,1024]{1,0:T(8,128)}) custom-call(s32[1]{0:T(128)} %bitcast.7.place_ref, s16[8,1040,128]{2,1,0:T(8,128)(2,1)S(1)} %bitcast.13, f32[128,1024]{1,0:T(8,128)S(1)} %bitcast.19, f32[128,1024]{1,0:T(8,128)S(1)} %bitcast.20), custom_call_target="tpu_custom_call" | custom-call | flops 1610612736 | bytes 6291456 | tf_op jit(solution)/shard_map/stats/pallas_call | solution.py:239
  162.9 7.1 %all-to-all-done.2 = bf16[64,16,128]{2,1,0:T(8,128)(2,1)S(1)} async-done(((bf16[64,16,128]{2,1,0:T(8,128)(2,1)}), bf16[64,16,128]{2,1,0:T(8,128)(2,1)S(1)}, u32[]{:S(2)}, u32[]{:S(2)}) %all-to-all-start.2) | async-done | bytes 262176 | tf_op jit(solution)/shard_map/all_to_all | solution.py:272
  170.0 1.3 gather_fusion
  (8 shorter events, 0.0 us)
Async XLA Ops:
  7.2 1.6 copy-start.1
  8.8 0.7 copy-start.4
  13.6 1.3 copy-start
  15.0 76.3 %all-to-all-start = ((bf16[512,16,128]{2,1,0:T(8,128)(2,1)}), bf16[512,16,128]{2,1,0:T(8,128)(2,1)S(1)}, u32[]{:S(2)}, u32[]{:S(2)}) async-start(bf16[512,16,128]{2,1,0:T(8,128)(2,1)} %bitcast.15), calls=%async_computation | async-start | bytes 4194304 | tf_op jit(solution)/shard_map/all_to_all | solution.py:265
  37.1 89.9 %all-gather.5.cloned.1.call-start = ((), (), s32[]{:S(2)}) async-start(), calls=%async_computation.3 | async-start | bytes 2359296 | tf_op jit(solution)/shard_map/all_gather | solution.py:262
  91.3 35.7 %copy-start.3 = (bf16[1,128,1024]{2,1,0:T(8,128)(2,1)S(1)}, bf16[1,128,1024]{2,1,0:T(8,128)(2,1)}, u32[]{:S(2)}) copy-start(bf16[1,128,1024]{2,1,0:T(8,128)(2,1)} %param.11) | copy-start | bytes 786436
  127.0 1.6 copy-start.2
  128.6 28.3 %copy-start.5 = (s32[64]{0:T(128)S(1)}, s32[64]{0:T(128)}, u32[]{:S(2)}) copy-start(s32[64]{0:T(128)} %assign_ref.1) | copy-start | bytes 772
  128.6 28.3 %copy-start.6 = (f32[1,128,1024]{2,1,0:T(8,128)S(1)}, f32[1,128,1024]{2,1,0:T(8,128)}, u32[]{:S(2)}) copy-start(f32[1,128,1024]{2,1,0:T(8,128)} %param.8) | copy-start | bytes 1572868
  128.6 28.3 %copy-start.7 = (f32[1,128,1024]{2,1,0:T(8,128)S(1)}, f32[1,128,1024]{2,1,0:T(8,128)}, u32[]{:S(2)}) copy-start(f32[1,128,1024]{2,1,0:T(8,128)} %param.9) | copy-start | bytes 1572868
  143.8 26.2 %all-to-all-start.2 = ((bf16[64,16,128]{2,1,0:T(8,128)(2,1)}), bf16[64,16,128]{2,1,0:T(8,128)(2,1)S(1)}, u32[]{:S(2)}, u32[]{:S(2)}) async-start(bf16[64,16,128]{2,1,0:T(8,128)(2,1)} %bitcast.6), calls=%async_computation.2 | async-start | bytes 524288 | tf_op jit(solution)/shard_map/all_to_all | solution.py:272
Sparse Core Ops, SparseCore 0:
  40.0 76.2 all-gather.4

commit v3 on v2

--- a/solution.py
+++ b/solution.py
@@ -13,6 +13,7 @@
 TOP = 32767.0
 FLOOR = 1e-30
 CODES = 16
+BITS = (64, 32, 16, 8, 4, 2, 1)
 MIB = 1 << 20
 
 
@@ -50,7 +51,7 @@
             pltpu.make_async_copy(turned.at[b], out_ref.at[assign_ref[b]], out_sem).start()
             return carry
 
-        lax.fori_loop(c * chunk, (c + 1) * chunk, turn, 0)
+        lax.fori_loop(c * chunk, (c + 1) * chunk, turn, 0, unroll=True)
     pltpu.make_async_copy(turned, out_ref, out_sem).wait()
 
 
@@ -65,10 +66,10 @@
         scratch_shapes=[
             pltpu.VMEM(grads.shape, grads.dtype),
             pltpu.VMEM(shape, grads.dtype),
-            pltpu.SemaphoreType.DMA((4,)),
+            pltpu.SemaphoreType.DMA((8,)),
             pltpu.SemaphoreType.DMA,
         ],
-        compiler_params=pltpu.CompilerParams(vmem_limit_bytes=16 * MIB),
+        compiler_params=pltpu.CompilerParams(vmem_limit_bytes=60 * MIB),
         cost_estimate=cost(0, 2 * grads.size * 2),
         name="send",
     )(assign, grads)
@@ -78,7 +79,7 @@
     return jnp.exp(code * (1.0 / STEPS)) * (1.0 / TOP)
 
 
-def fold_kernel(arrived_ref, packed_ref):
+def fold_kernel(arrived_ref, root_ref, packed_ref):
     shards, replicas, rows, width = arrived_ref.shape
     group = shards // CODES
     codes = []
@@ -93,24 +94,25 @@
         codes.append(code)
     codes = jnp.concatenate(codes, axis=0).astype(jnp.int32).astype(jnp.int16)
     packed_ref[pl.ds(shards * rows, CODES), :] = codes
-
-
-def fold(arrived):
+    packed_ref[pl.ds(shards * rows + CODES, root_ref.shape[0]), :] = root_ref[...]
+
+
+def fold(arrived, root):
     shards, replicas, rows, width = arrived.shape
     return pl.pallas_call(
         fold_kernel,
-        out_shape=jax.ShapeDtypeStruct((shards * rows + CODES, width), jnp.int16),
-        in_specs=[vmem()],
+        out_shape=jax.ShapeDtypeStruct((shards * rows + CODES + root.shape[0], width), jnp.int16),
+        in_specs=[vmem()] * 2,
         out_specs=vmem(),
         compiler_params=pltpu.CompilerParams(vmem_limit_bytes=16 * MIB),
         cost_estimate=cost(arrived.size, 2 * arrived.size),
         name="fold",
-    )(arrived)
+    )(arrived, root)
 
 
 def unpack(spread_ref, k, high, low):
     width = spread_ref.shape[2]
-    size = spread_ref.shape[1] - CODES
+    size = high.shape[0]
     rows = size // CODES
     columns = pl.ds(k * width, width)
     scales = scale_of(spread_ref[k, pl.ds(size, CODES), :].astype(jnp.int32).astype(jnp.float32))
@@ -126,6 +128,24 @@
     return square
 
 
+def decode(spread_ref, i, left):
+    slabs, rows, size = spread_ref.shape
+    start = left.shape[0] + CODES
+    for d in range((rows - start) // size):
+        code = spread_ref[i, pl.ds(start + d * size, size), :].astype(jnp.int32)
+        count = jnp.abs(code) - 1
+        depth = lax.shift_right_arithmetic(count, 7)
+        value = ((count & 127) + 128).astype(jnp.float32) * (1.0 / 64.0)
+        for bit in BITS:
+            value = jnp.where((depth & bit) != 0, value * (2.0**-bit), value)
+        value = jnp.where(code < 0, -value, value)
+        value = jnp.where(code == 0, 0.0, value)
+        j = (i + d) % slabs
+        left[pl.ds(i * size, size), pl.ds(j * size, size)] = value.astype(jnp.bfloat16)
+        if 0 < d < slabs - d:
+            left[pl.ds(j * size, size), pl.ds(i * size, size)] = value.T.astype(jnp.bfloat16)
+
+
 NT = (((1,), (1,)), ((), ()))
 NN = (((1,), (0,)), ((), ()))
 
@@ -134,13 +154,14 @@
     return lax.dot_general(a, b, dims, preferred_element_type=jnp.float32)
 
 
-def shape_kernel(spread_ref, left_ref, right_ref, out_ref, squares_ref, total_ref, high, low, mid):
+def shape_kernel(spread_ref, right_ref, out_ref, squares_ref, total_ref, high, low, mid, left_ref):
     slabs = spread_ref.shape[0]
     size, width = out_ref.shape
     tile = 256
     square = jnp.zeros((8, width), jnp.float32)
     for k in range(slabs):
         square = square + unpack(spread_ref, k, high, low)
+        decode(spread_ref, k, left_ref)
     total_ref[...] = square
 
     def right_step(t, carry):
@@ -161,38 +182,38 @@
         return square + jnp.sum((part * part).reshape(tile // 8, 8, width), axis=0)
 
     square = lax.fori_loop(0, size // tile, left_step, jnp.zeros((8, width), jnp.float32))
-    for k in range(slabs):
-        squares_ref[k] = square
-
-
-def shape(spread, left, right):
+    squares_ref[...] = jnp.broadcast_to(jnp.sum(square, axis=0, keepdims=True), (slabs, width))
+
+
+def shape(spread, right):
     slabs, _, width = spread.shape
-    size = left.shape[0]
+    size = right.shape[1]
     return pl.pallas_call(
         shape_kernel,
         out_shape=(
             jax.ShapeDtypeStruct((size, width), jnp.float32),
-            jax.ShapeDtypeStruct((slabs, 8, width), jnp.float32),
+            jax.ShapeDtypeStruct((slabs, width), jnp.float32),
             jax.ShapeDtypeStruct((8, width), jnp.float32),
         ),
-        in_specs=[vmem()] * 3,
+        in_specs=[vmem()] * 2,
         out_specs=(vmem(),) * 3,
         scratch_shapes=[
             pltpu.VMEM((size, size), jnp.bfloat16),
             pltpu.VMEM((size, size), jnp.bfloat16),
             pltpu.VMEM((size, 2 * width), jnp.bfloat16),
+            pltpu.VMEM((size, size), jnp.bfloat16),
         ],
         compiler_params=pltpu.CompilerParams(vmem_limit_bytes=24 * MIB),
         cost_estimate=cost(8 * size * size * width, 6 * size * size),
         name="shape",
-    )(spread, left, right)
+    )(spread, right)
 
 
 def graft_kernel(shaped_ref, squares_ref, total_ref, out_ref):
     def whole(x):
         return jnp.sum(jnp.sum(x, axis=0, keepdims=True), axis=1, keepdims=True)
 
-    shaped_square = whole(jnp.sum(squares_ref[...], axis=0))
+    shaped_square = whole(squares_ref[...])
     block_square = whole(total_ref[...])
     ratio = jnp.sqrt((block_square + EPSILON) / (shaped_square + EPSILON))
     out_ref[...] = (shaped_ref[...] * ratio).astype(jnp.bfloat16)
@@ -252,6 +273,38 @@
     )(place, spread, left, right)
 
 
+def encode_kernel(place_ref, left_ref, code_ref):
+    size = left_ref.shape[0]
+    slabs = left_ref.shape[1] // size
+    for d in range(code_ref.shape[0] // size):
+        column = lax.rem(place_ref[0] + d, slabs) * size
+        value = left_ref[:, pl.ds(pl.multiple_of(column, size), size)].astype(jnp.float32)
+        rest = jnp.abs(value)
+        depth = jnp.zeros(value.shape, jnp.float32)
+        for bit in BITS:
+            scaled = rest * (2.0**bit)
+            keep = scaled < 4.0
+            rest = jnp.where(keep, scaled, rest)
+            depth = jnp.where(keep, depth + bit, depth)
+        code = jnp.where(value == 0.0, 0.0, depth * 128.0 + rest * 64.0 - 127.0)
+        code = jnp.where(value < 0.0, -code, code)
+        code_ref[pl.ds(d * size, size), :] = code.astype(jnp.int32).astype(jnp.int16)
+
+
+def encode(place, left, slabs):
+    rows = left.shape[0]
+    count = slabs // 2 + 1
+    return pl.pallas_call(
+        encode_kernel,
+        out_shape=jax.ShapeDtypeStruct((count * rows, rows), jnp.int16),
+        in_specs=[pl.BlockSpec(memory_space=pltpu.SMEM), vmem()],
+        out_specs=vmem(),
+        compiler_params=pltpu.CompilerParams(vmem_limit_bytes=8 * MIB),
+        cost_estimate=cost(30 * count * rows * rows, 4 * left.size),
+        name="encode",
+    )(place, left)
+
+
 def body(grads, assign, left_factor, right_factor, left_root, right_root):
     fsdp_size = lax.axis_size("fsdp")
     dp_size = lax.axis_size("dp")
@@ -259,13 +312,14 @@
     width = grads.shape[3]
     col_width = width // dp_size
     place = lax.axis_index("dp").astype(jnp.int32).reshape(1)
-    left_full = lax.all_gather(left_root[0], "dp", axis=0, tiled=True)
     outgoing = send(assign, grads[0], dp_size)
     outgoing = outgoing.reshape(fsdp_size * dp_size, shard_rows, col_width)
+    outgoing, left_rows = lax.optimization_barrier((outgoing, left_root[0]))
+    codes = encode(place, left_rows, dp_size)
     arrived = lax.all_to_all(outgoing, ("fsdp", "dp"), split_axis=0, concat_axis=0, tiled=True)
-    packed = fold(arrived.reshape(fsdp_size, dp_size, shard_rows, col_width))
+    packed = fold(arrived.reshape(fsdp_size, dp_size, shard_rows, col_width), codes)
     spread = lax.all_gather(packed, "dp", axis=0)
-    shaped, squares, total = shape(spread, left_full, right_root[0])
+    shaped, squares, total = shape(spread, right_root[0])
     squares = lax.all_to_all(squares, "dp", split_axis=0, concat_axis=0, tiled=True)
     rounded = graft(shaped, squares, total).reshape(fsdp_size, shard_rows, col_width)
     rounded, spread = lax.optimization_barrier((rounded, spread))

time: 179 us -> 160 us (0.89)
  between operations: 14.1 us -> 0.74 us
  starting transfers between devices: 35.2 us -> 31 us
  Pallas kernels: 16.1 us -> 18.9 us
  waiting for transfers between devices: 61.2 us -> 58.5 us
    all_to_all x1, starting transfers between devices: 13 us -> 8.84 us  [body(): lax.all_to_all(rounded, 'fsdp', split_axis=0, concat_axis=0, tiled=True)]
    pallas_call x1, Pallas kernels: 4.54 us -> 8.7 us  [shape(): pl.pallas_call(shape_kernel, out_shape=(jax.ShapeDtypeStruct((size, width...]
    unnamed x16 -> x12, local copies, waits for them, and re-layouts: 5.17 us -> 2.79 us
    all_to_all x1, waiting for transfers between devices: 7.09 us -> 4.94 us  [body(): lax.all_to_all(rounded, 'fsdp', split_axis=0, concat_axis=0, tiled=True)]
  transfers between devices with their start and end apart: 3 -> 2, of which waited for: 2 -> 2; matrix products, arithmetic and copies ran while one was open for 0% -> 0% of each run, Pallas kernels for 4% -> 4%
where the time goes in v3:
time: 160 us
  waiting for transfers between devices  58.5 us (37%)
  blocking collectives  45.6 us (28%)
  starting transfers between devices  31 us (19%)
  Pallas kernels  18.9 us (12%)
  local copies, waits for them, and re-layouts  5.06 us (3%)
    all_to_all x1, waiting for transfers between devices, body(): lax.all_to_all(outgoing, ('fsdp', 'dp'), split_axis=0, concat_axis=0, til...  53.6 us
    all_gather x1, blocking collectives, body(): spread = lax.all_gather(packed, 'dp', axis=0)  36 us
    all_to_all x1, starting transfers between devices, body(): lax.all_to_all(outgoing, ('fsdp', 'dp'), split_axis=0, concat_axis=0, til...  22.2 us
    all_to_all x1, blocking collectives, body(): lax.all_to_all(squares, 'dp', split_axis=0, concat_axis=0, tiled=True)  9.68 us
    all_to_all x1, starting transfers between devices, body(): lax.all_to_all(rounded, 'fsdp', split_axis=0, concat_axis=0, tiled=True)  8.84 us
    pallas_call x1, Pallas kernels, shape(): pl.pallas_call(shape_kernel, out_shape=(jax.ShapeDtypeStruct((size, width...  8.7 us
    pallas_call x1, Pallas kernels, stats(): pl.pallas_call(stats_kernel, out_shape=(jax.ShapeDtypeStruct(left.shape,...  6.02 us
    all_to_all x1, waiting for transfers between devices, body(): lax.all_to_all(rounded, 'fsdp', split_axis=0, concat_axis=0, tiled=True)  4.94 us
  transfers between devices with their start and end apart: 2, of which 2 were waited for; matrix products, arithmetic and copies ran while one was open for 0% of the time, Pallas kernels for 4%

profile of v3, /device:TPU:1, one launch (start us, length us, event | category | flops | bytes accessed | tf_op | source)
XLA Modules:
  0.0 159.9 jit_solution(12860356550819945455)
XLA Ops:
  0.6 3.0 %send.1 = bf16[64,8,16,128]{3,2,1,0:T(8,128)(2,1)} custom-call(s32[64]{0:T(128)} %assign_ref.1, bf16[64,16,1024]{2,1,0:T(8,128)(2,1)} %bitcast.27), custom_call_target="tpu_custom_call" | custom-call | bytes 4194304 | tf_op jit(solution)/shard_map/send/pallas_call | solution.py:61
  3.7 0.0 copy-start.1
  3.7 22.2 %all-to-all-start = ((bf16[512,16,128]{2,1,0:T(8,128)(2,1)}), bf16[512,16,128]{2,1,0:T(8,128)(2,1)S(1)}, u32[]{:S(2)}, u32[]{:S(2)}) async-start(bf16[512,16,128]{2,1,0:T(8,128)(2,1)} %bitcast.26), calls=%async_computation | async-start | bytes 4194304 | tf_op jit(solution)/shard_map/all_to_all | solution.py:319
  25.9 0.0 copy-done.1
  25.9 0.5 encode.1.root_ref
  26.4 53.6 %all-to-all-done = bf16[512,16,128]{2,1,0:T(8,128)(2,1)S(1)} async-done(((bf16[512,16,128]{2,1,0:T(8,128)(2,1)}), bf16[512,16,128]{2,1,0:T(8,128)(2,1)S(1)}, u32[]{:S(2)}, u32[]{:S(2)}) %all-to-all-start) | async-done | bytes 2097184 | tf_op jit(solution)/shard_map/all_to_all | solution.py:319
  80.0 0.5 fold.1
  80.5 0.0 copy-start.4
  80.5 36.0 %all-gather.2 = s16[13440,128]{1,0:T(8,128)(2,1)S(1)} all-gather(s16[1680,128]{1,0:T(8,128)(2,1)S(1)} %fold.1), channel_id=2, replica_groups=mesh['fsdp'=64,'dp'=8] {'dp'}, dimensions={0}, use_global_device_ids=true | all-gather | bytes 3870720 | tf_op jit(solution)/shard_map/all_gather | solution.py:321
  116.4 0.0 copy-done.4
  116.4 0.0 copy-start.5
  116.4 8.7 %shape.1 = (f32[1024,128]{1,0:T(8,128)S(1)}, f32[8,128]{1,0:T(8,128)S(1)}, f32[8,128]{1,0:T(8,128)S(1)}) custom-call(s16[8,1680,128]{2,1,0:T(8,128)(2,1)S(1)} %bitcast.17, bf16[128,1024]{1,0:T(8,128)(2,1)S(1)} %bitcast.25), custom_call_target="tpu_custom_call" | custom-call | flops 1073741824 | bytes 6291456 | tf_op jit(solution)/shard_map/shape/pallas_call | solution.py:191
  125.1 9.7 %all_to_all.21 = f32[8,1,128]{2,1,0:T(1,128)S(1)} all-to-all(f32[8,1,128]{2,1,0:T(1,128)S(1)} %bitcast.22), channel_id=1, replica_groups=mesh['fsdp'=64,'dp'=8] {'dp'}, dimensions={0} | all-to-all | bytes 8192 | tf_op jit(solution)/shard_map/all_to_all | solution.py:323
  134.8 0.1 graft.1
  135.0 0.0 copy-start
  135.0 0.7 copy-done
  135.7 8.8 %all-to-all-start.2 = ((bf16[64,16,128]{2,1,0:T(8,128)(2,1)}), bf16[64,16,128]{2,1,0:T(8,128)(2,1)}, u32[]{:S(2)}, u32[]{:S(2)}) async-start(bf16[64,16,128]{2,1,0:T(8,128)(2,1)} %bitcast.19), calls=%async_computation.2 | async-start | bytes 524288 | tf_op jit(solution)/shard_map/all_to_all | solution.py:326
  144.5 0.0 copy-done.5
  144.5 0.0 copy-start.2
  144.6 1.0 copy-done.2
  145.6 1.0 copy-done.3
  146.6 6.0 %stats.1 = (f32[128,1024]{1,0:T(8,128)}, f32[128,1024]{1,0:T(8,128)}) custom-call(s32[1]{0:T(128)} %bitcast.4.place_ref, s16[8,1680,128]{2,1,0:T(8,128)(2,1)S(1)} %bitcast.18, f32[128,1024]{1,0:T(8,128)S(1)} %bitcast.23, f32[128,1024]{1,0:T(8,128)S(1)} %bitcast.24), custom_call_target="tpu_custom_call" | custom-call | flops 1610612736 | bytes 6291456 | tf_op jit(solution)/shard_map/stats/pallas_call | solution.py:260
  152.7 4.9 %all-to-all-done.2 = bf16[64,16,128]{2,1,0:T(8,128)(2,1)} async-done(((bf16[64,16,128]{2,1,0:T(8,128)(2,1)}), bf16[64,16,128]{2,1,0:T(8,128)(2,1)}, u32[]{:S(2)}, u32[]{:S(2)}) %all-to-all-start.2) | async-done | bytes 262176 | tf_op jit(solution)/shard_map/all_to_all | solution.py:326
  157.6 2.3 %gather_fusion = bf16[64,16,128]{2,1,0:T(8,128)(2,1)} fusion(bf16[64,16,128]{2,1,0:T(8,128)(2,1)} %all-to-all-done.2, s32[1024]{0:T(1024)S(1)} %pad_clamp_fusion), kind=kCustom, calls=%fused_computation | custom fusion | bytes 524544 | tf_op jit(solution)/shard_map/jit(_take)/gather | solution.py:328
  (2 shorter events, 0.0 us)
Async XLA Ops:
  3.7 22.2 %copy-start.1 = (bf16[1,128,1024]{2,1,0:T(8,128)(2,1)S(1)}, bf16[1,128,1024]{2,1,0:T(8,128)(2,1)}, u32[]{:S(2)}) copy-start(bf16[1,128,1024]{2,1,0:T(8,128)(2,1)} %param.10) | copy-start | bytes 786436
  3.7 76.3 %all-to-all-start = ((bf16[512,16,128]{2,1,0:T(8,128)(2,1)}), bf16[512,16,128]{2,1,0:T(8,128)(2,1)S(1)}, u32[]{:S(2)}, u32[]{:S(2)}) async-start(bf16[512,16,128]{2,1,0:T(8,128)(2,1)} %bitcast.26), calls=%async_computation | async-start | bytes 4194304 | tf_op jit(solution)/shard_map/all_to_all | solution.py:319
  80.5 36.0 %copy-start.4 = (bf16[1,128,1024]{2,1,0:T(8,128)(2,1)S(1)}, bf16[1,128,1024]{2,1,0:T(8,128)(2,1)}, u32[]{:S(2)}) copy-start(bf16[1,128,1024]{2,1,0:T(8,128)(2,1)} %param.11) | copy-start | bytes 786436
  116.4 28.1 %copy-start.5 = (s32[64]{0:T(128)S(1)}, s32[64]{0:T(128)}, u32[]{:S(2)}) copy-start(s32[64]{0:T(128)} %assign_ref.1) | copy-start | bytes 772
  135.0 0.7 copy-start
  135.7 21.9 %all-to-all-start.2 = ((bf16[64,16,128]{2,1,0:T(8,128)(2,1)}), bf16[64,16,128]{2,1,0:T(8,128)(2,1)}, u32[]{:S(2)}, u32[]{:S(2)}) async-start(bf16[64,16,128]{2,1,0:T(8,128)(2,1)} %bitcast.19), calls=%async_computation.2 | async-start | bytes 524288 | tf_op jit(solution)/shard_map/all_to_all | solution.py:326
  144.5 1.0 copy-start.2
  145.6 1.0 copy-start.3

commit v4 on v3

--- a/solution.py
+++ b/solution.py
@@ -79,10 +79,11 @@
     return jnp.exp(code * (1.0 / STEPS)) * (1.0 / TOP)
 
 
-def fold_kernel(arrived_ref, root_ref, packed_ref):
+def fold_kernel(arrived_ref, root_ref, packed_ref, square_ref):
     shards, replicas, rows, width = arrived_ref.shape
     group = shards // CODES
     codes = []
+    square = jnp.zeros((8, width), jnp.float32)
     for g in range(CODES):
         terms = arrived_ref[pl.ds(g * group, group)].astype(jnp.float32)
         total = jnp.sum(terms, axis=1).reshape(group * rows, width)
@@ -92,6 +93,8 @@
         units = jnp.clip(units, -TOP, TOP).astype(jnp.int32).astype(jnp.int16)
         packed_ref[pl.ds(g * group * rows, group * rows), :] = units
         codes.append(code)
+        square = square + jnp.sum((total * total).reshape(group * rows // 8, 8, width), axis=0)
+    square_ref[...] = square
     codes = jnp.concatenate(codes, axis=0).astype(jnp.int32).astype(jnp.int16)
     packed_ref[pl.ds(shards * rows, CODES), :] = codes
     packed_ref[pl.ds(shards * rows + CODES, root_ref.shape[0]), :] = root_ref[...]
@@ -101,9 +104,12 @@
     shards, replicas, rows, width = arrived.shape
     return pl.pallas_call(
         fold_kernel,
-        out_shape=jax.ShapeDtypeStruct((shards * rows + CODES + root.shape[0], width), jnp.int16),
+        out_shape=(
+            jax.ShapeDtypeStruct((shards * rows + CODES + root.shape[0], width), jnp.int16),
+            jax.ShapeDtypeStruct((8, width), jnp.float32),
+        ),
         in_specs=[vmem()] * 2,
-        out_specs=vmem(),
+        out_specs=(vmem(),) * 2,
         compiler_params=pltpu.CompilerParams(vmem_limit_bytes=16 * MIB),
         cost_estimate=cost(arrived.size, 2 * arrived.size),
         name="fold",
@@ -116,7 +122,6 @@
     rows = size // CODES
     columns = pl.ds(k * width, width)
     scales = scale_of(spread_ref[k, pl.ds(size, CODES), :].astype(jnp.int32).astype(jnp.float32))
-    square = jnp.zeros((8, width), jnp.float32)
     for g in range(CODES):
         here = pl.ds(g * rows, rows)
         units = spread_ref[k, here, :].astype(jnp.int32).astype(jnp.float32)
@@ -124,8 +129,6 @@
         upper = values.astype(jnp.bfloat16)
         high[here, columns] = upper
         low[here, columns] = (values - upper.astype(jnp.float32)).astype(jnp.bfloat16)
-        square = square + jnp.sum((values * values).reshape(rows // 8, 8, width), axis=0)
-    return square
 
 
 def decode(spread_ref, i, left):
@@ -134,16 +137,14 @@
     for d in range((rows - start) // size):
         code = spread_ref[i, pl.ds(start + d * size, size), :].astype(jnp.int32)
         count = jnp.abs(code) - 1
-        depth = lax.shift_right_arithmetic(count, 7)
-        value = ((count & 127) + 128).astype(jnp.float32) * (1.0 / 64.0)
-        for bit in BITS:
-            value = jnp.where((depth & bit) != 0, value * (2.0**-bit), value)
+        power = jnp.exp2((1 - lax.shift_right_arithmetic(count, 7)).astype(jnp.float32))
+        value = ((count & 127) + 128).astype(jnp.float32) * (1.0 / 128.0) * power
         value = jnp.where(code < 0, -value, value)
-        value = jnp.where(code == 0, 0.0, value)
+        value = jnp.where(code == 0, 0.0, value).astype(jnp.bfloat16)
         j = (i + d) % slabs
-        left[pl.ds(i * size, size), pl.ds(j * size, size)] = value.astype(jnp.bfloat16)
+        left[pl.ds(i * size, size), pl.ds(j * size, size)] = value
         if 0 < d < slabs - d:
-            left[pl.ds(j * size, size), pl.ds(i * size, size)] = value.T.astype(jnp.bfloat16)
+            left[pl.ds(j * size, size), pl.ds(i * size, size)] = value.T
 
 
 NT = (((1,), (1,)), ((), ()))
@@ -154,15 +155,21 @@
     return lax.dot_general(a, b, dims, preferred_element_type=jnp.float32)
 
 
-def shape_kernel(spread_ref, right_ref, out_ref, squares_ref, total_ref, high, low, mid, left_ref):
+def halves(a, b):
+    a, b = (jnp.sum(x, axis=0, keepdims=True) for x in (a, b))
+    width = a.shape[1]
+    lane = lax.broadcasted_iota(jnp.int32, a.shape, 1)
+    a, b = (x + pltpu.roll(x, width // 2, 1) for x in (a, b))
+    return jnp.where(lane < width // 2, a, b)
+
+
+def shape_kernel(spread_ref, right_ref, square_ref, out_ref, squares_ref, high, low, mid, left_ref):
     slabs = spread_ref.shape[0]
     size, width = out_ref.shape
     tile = 256
-    square = jnp.zeros((8, width), jnp.float32)
     for k in range(slabs):
-        square = square + unpack(spread_ref, k, high, low)
+        unpack(spread_ref, k, high, low)
         decode(spread_ref, k, left_ref)
-    total_ref[...] = square
 
     def right_step(t, carry):
         rows = pl.ds(pl.multiple_of(t * tile, tile), tile)
@@ -174,18 +181,16 @@
 
     lax.fori_loop(0, size // tile, right_step, 0)
 
-    def left_step(t, square):
-        rows = pl.ds(pl.multiple_of(t * tile, tile), tile)
-        both = dot(left_ref[rows, :], mid[...], NN)
+    square = jnp.zeros((8, width), jnp.float32)
+    for t in range(size // tile):
+        both = dot(left_ref[pl.ds(t * tile, tile), :], mid[...], NN)
         part = both[:, :width] + both[:, width:]
-        out_ref[rows, :] = part
-        return square + jnp.sum((part * part).reshape(tile // 8, 8, width), axis=0)
-
-    square = lax.fori_loop(0, size // tile, left_step, jnp.zeros((8, width), jnp.float32))
-    squares_ref[...] = jnp.broadcast_to(jnp.sum(square, axis=0, keepdims=True), (slabs, width))
-
-
-def shape(spread, right):
+        square = square + jnp.sum((part * part).reshape(tile // 8, 8, width), axis=0)
+        out_ref[pl.ds(t * tile, tile), :] = part
+    squares_ref[...] = jnp.broadcast_to(halves(square, square_ref[...]), (slabs, width))
+
+
+def shape(spread, right, square):
     slabs, _, width = spread.shape
     size = right.shape[1]
     return pl.pallas_call(
@@ -193,10 +198,9 @@
         out_shape=(
             jax.ShapeDtypeStruct((size, width), jnp.float32),
             jax.ShapeDtypeStruct((slabs, width), jnp.float32),
-            jax.ShapeDtypeStruct((8, width), jnp.float32),
         ),
-        in_specs=[vmem()] * 2,
-        out_specs=(vmem(),) * 3,
+        in_specs=[vmem()] * 3,
+        out_specs=(vmem(),) * 2,
         scratch_shapes=[
             pltpu.VMEM((size, size), jnp.bfloat16),
             pltpu.VMEM((size, size), jnp.bfloat16),
@@ -206,29 +210,45 @@
         compiler_params=pltpu.CompilerParams(vmem_limit_bytes=24 * MIB),
         cost_estimate=cost(8 * size * size * width, 6 * size * size),
         name="shape",
-    )(spread, right)
-
-
-def graft_kernel(shaped_ref, squares_ref, total_ref, out_ref):
-    def whole(x):
-        return jnp.sum(jnp.sum(x, axis=0, keepdims=True), axis=1, keepdims=True)
-
-    shaped_square = whole(squares_ref[...])
-    block_square = whole(total_ref[...])
+    )(spread, right, square)
+
+
+def graft_kernel(squares_ref, shaped_ref, out_ref):
+    total = jnp.sum(squares_ref[...], axis=0, keepdims=True)
+    first = lax.broadcasted_iota(jnp.int32, total.shape, 1) < total.shape[1] // 2
+    shaped_square = jnp.sum(jnp.where(first, total, 0.0), axis=1, keepdims=True)
+    block_square = jnp.sum(jnp.where(first, 0.0, total), axis=1, keepdims=True)
     ratio = jnp.sqrt((block_square + EPSILON) / (shaped_square + EPSILON))
     out_ref[...] = (shaped_ref[...] * ratio).astype(jnp.bfloat16)
 
 
-def graft(shaped, squares, total):
+def graft(squares, shaped):
     return pl.pallas_call(
         graft_kernel,
         out_shape=jax.ShapeDtypeStruct(shaped.shape, jnp.bfloat16),
-        in_specs=[vmem()] * 3,
+        in_specs=[vmem()] * 2,
         out_specs=vmem(),
         compiler_params=pltpu.CompilerParams(vmem_limit_bytes=8 * MIB),
         cost_estimate=cost(shaped.size, 6 * shaped.size),
         name="graft",
-    )(shaped, squares, total)
+    )(squares, shaped)
+
+
+def place_kernel(assign_ref, returned_ref, out_ref):
+    for b in range(out_ref.shape[0]):
+        out_ref[b] = returned_ref[assign_ref[b]]
+
+
+def place_blocks(assign, returned):
+    return pl.pallas_call(
+        place_kernel,
+        out_shape=jax.ShapeDtypeStruct(returned.shape, returned.dtype),
+        in_specs=[pl.BlockSpec(memory_space=pltpu.SMEM), vmem()],
+        out_specs=vmem(),
+        compiler_params=pltpu.CompilerParams(vmem_limit_bytes=8 * MIB),
+        cost_estimate=cost(0, 4 * returned.size),
+        name="place",
+    )(assign, returned)
 
 
 def stats_kernel(place_ref, spread_ref, left_ref, right_ref, left_out, right_out, high, low, turned):
@@ -317,15 +337,15 @@
     outgoing, left_rows = lax.optimization_barrier((outgoing, left_root[0]))
     codes = encode(place, left_rows, dp_size)
     arrived = lax.all_to_all(outgoing, ("fsdp", "dp"), split_axis=0, concat_axis=0, tiled=True)
-    packed = fold(arrived.reshape(fsdp_size, dp_size, shard_rows, col_width), codes)
+    packed, square = fold(arrived.reshape(fsdp_size, dp_size, shard_rows, col_width), codes)
     spread = lax.all_gather(packed, "dp", axis=0)
-    shaped, squares, total = shape(spread, right_root[0])
+    shaped, squares = shape(spread, right_root[0], square)
     squares = lax.all_to_all(squares, "dp", split_axis=0, concat_axis=0, tiled=True)
-    rounded = graft(shaped, squares, total).reshape(fsdp_size, shard_rows, col_width)
+    rounded = graft(squares, shaped).reshape(fsdp_size, shard_rows, col_width)
     rounded, spread = lax.optimization_barrier((rounded, spread))
     returned = lax.all_to_all(rounded, "fsdp", split_axis=0, concat_axis=0, tiled=True)
     left_out, right_out = stats(place, spread, left_factor[0], right_factor[0])
-    update = jnp.take(returned, assign, axis=0, mode="clip")
+    update = place_blocks(assign, returned)
     return (update, left_out[None], right_out[None])
 
 

time: 160 us -> 157 us (0.981)
  local copies, waits for them, and re-layouts: 5.06 us -> 2.79 us
    pallas_call x1, Pallas kernels: 8.7 us -> 5.89 us  [shape(): pl.pallas_call(shape_kernel, out_shape=(jax.ShapeDtypeStruct((size, width...]
    gather x1 -> x0, local copies, waits for them, and re-layouts: 2.27 us -> none  [body(): update = jnp.take(returned, assign, axis=0, mode='clip')]
    pallas_call x1 -> x2, Pallas kernels: 0.45 us -> 2.22 us  [the longest x1 1.72 us: place_blocks(): pl.pallas_call(place_kernel, out_shape=jax.ShapeDtypeStruct(returned.shap...]
where the time goes in v4:
time: 157 us
  waiting for transfers between devices  58.5 us (37%)
  blocking collectives  45.6 us (29%)
  starting transfers between devices  31 us (20%)
  Pallas kernels  17.8 us (11%)
  local copies, waits for them, and re-layouts  2.79 us (2%)
    all_to_all x1, waiting for transfers between devices, body(): lax.all_to_all(outgoing, ('fsdp', 'dp'), split_axis=0, concat_axis=0, til...  53.6 us
    all_gather x1, blocking collectives, body(): spread = lax.all_gather(packed, 'dp', axis=0)  36 us
    all_to_all x1, starting transfers between devices, body(): lax.all_to_all(outgoing, ('fsdp', 'dp'), split_axis=0, concat_axis=0, til...  22.2 us
    all_to_all x1, blocking collectives, body(): lax.all_to_all(squares, 'dp', split_axis=0, concat_axis=0, tiled=True)  9.67 us
    all_to_all x1, starting transfers between devices, body(): lax.all_to_all(rounded, 'fsdp', split_axis=0, concat_axis=0, tiled=True)  8.84 us
    pallas_call x1, Pallas kernels, stats(): pl.pallas_call(stats_kernel, out_shape=(jax.ShapeDtypeStruct(left.shape,...  6.03 us
    pallas_call x1, Pallas kernels, shape(): pl.pallas_call(shape_kernel, out_shape=(jax.ShapeDtypeStruct((size, width...  5.89 us
    all_to_all x1, waiting for transfers between devices, body(): lax.all_to_all(rounded, 'fsdp', split_axis=0, concat_axis=0, tiled=True)  4.96 us
  transfers between devices with their start and end apart: 2, of which 2 were waited for; matrix products, arithmetic and copies ran while one was open for 0% of the time, Pallas kernels for 4%

profile of v4, /device:TPU:1, one launch (start us, length us, event | category | flops | bytes accessed | tf_op | source)
XLA Modules:
  0.0 156.6 jit_solution(8712320542375908721)
XLA Ops:
  0.6 3.0 %send.1 = bf16[64,8,16,128]{3,2,1,0:T(8,128)(2,1)} custom-call(s32[64]{0:T(128)} %assign_ref.3, bf16[64,16,1024]{2,1,0:T(8,128)(2,1)} %bitcast.27), custom_call_target="tpu_custom_call" | custom-call | bytes 4194304 | tf_op jit(solution)/shard_map/send/pallas_call | solution.py:61
  3.7 0.0 copy-start.1
  3.7 22.2 %all-to-all-start = ((bf16[512,16,128]{2,1,0:T(8,128)(2,1)}), bf16[512,16,128]{2,1,0:T(8,128)(2,1)S(1)}, u32[]{:S(2)}, u32[]{:S(2)}) async-start(bf16[512,16,128]{2,1,0:T(8,128)(2,1)} %bitcast.26), calls=%async_computation | async-start | bytes 4194304 | tf_op jit(solution)/shard_map/all_to_all | solution.py:339
  25.9 0.0 copy-done.1
  25.9 0.5 encode.1.root_ref
  26.4 53.6 %all-to-all-done = bf16[512,16,128]{2,1,0:T(8,128)(2,1)S(1)} async-done(((bf16[512,16,128]{2,1,0:T(8,128)(2,1)}), bf16[512,16,128]{2,1,0:T(8,128)(2,1)S(1)}, u32[]{:S(2)}, u32[]{:S(2)}) %all-to-all-start) | async-done | bytes 2097184 | tf_op jit(solution)/shard_map/all_to_all | solution.py:339
  80.0 0.5 fold.1
  80.5 0.0 copy-start.5
  80.5 36.0 %all-gather.2 = s16[13440,128]{1,0:T(8,128)(2,1)S(1)} all-gather(s16[1680,128]{1,0:T(8,128)(2,1)S(1)} %get-tuple-element.15), channel_id=2, replica_groups=mesh['fsdp'=64,'dp'=8] {'dp'}, dimensions={0}, use_global_device_ids=true | all-gather | bytes 3870720 | tf_op jit(solution)/shard_map/all_gather | solution.py:341
  116.5 0.0 copy-done.5
  116.5 5.9 %shape.1 = (f32[1024,128]{1,0:T(8,128)S(1)}, f32[8,128]{1,0:T(8,128)S(1)}) custom-call(s16[8,1680,128]{2,1,0:T(8,128)(2,1)S(1)} %bitcast.17, bf16[128,1024]{1,0:T(8,128)(2,1)S(1)} %bitcast.25, f32[8,128]{1,0:T(8,128)S(1)} %get-tuple-element.16.square_ref), custom_call_target="tpu_custom_call" | custom-call | flops 1073741824 | bytes 6291456 | tf_op jit(solution)/shard_map/shape/pallas_call | solution.py:196
  122.4 9.7 %all_to_all.21 = f32[8,1,128]{2,1,0:T(1,128)S(1)} all-to-all(f32[8,1,128]{2,1,0:T(1,128)S(1)} %bitcast.22), channel_id=1, replica_groups=mesh['fsdp'=64,'dp'=8] {'dp'}, dimensions={0} | all-to-all | bytes 8192 | tf_op jit(solution)/shard_map/all_to_all | solution.py:343
  132.1 0.1 graft.1
  132.2 0.0 copy-start
  132.2 0.7 copy-done
  132.9 8.8 %all-to-all-start.2 = ((bf16[64,16,128]{2,1,0:T(8,128)(2,1)}), bf16[64,16,128]{2,1,0:T(8,128)(2,1)}, u32[]{:S(2)}, u32[]{:S(2)}) async-start(bf16[64,16,128]{2,1,0:T(8,128)(2,1)} %bitcast.19), calls=%async_computation.2 | async-start | bytes 524288 | tf_op jit(solution)/shard_map/all_to_all | solution.py:346
  141.8 0.0 copy-start.3
  141.8 1.0 copy-done.3
  142.8 0.0 copy-start.4
  142.8 1.0 copy-done.4
  143.9 6.0 %stats.1 = (f32[128,1024]{1,0:T(8,128)}, f32[128,1024]{1,0:T(8,128)}) custom-call(s32[1]{0:T(128)} %bitcast.4.place_ref, s16[8,1680,128]{2,1,0:T(8,128)(2,1)S(1)} %bitcast.18, f32[128,1024]{1,0:T(8,128)S(1)} %bitcast.23, f32[128,1024]{1,0:T(8,128)S(1)} %bitcast.24), custom_call_target="tpu_custom_call" | custom-call | flops 1610612736 | bytes 6291456 | tf_op jit(solution)/shard_map/stats/pallas_call | solution.py:280
  149.9 5.0 %all-to-all-done.2.returned_ref = bf16[64,16,128]{2,1,0:T(8,128)(2,1)} async-done(((bf16[64,16,128]{2,1,0:T(8,128)(2,1)}), bf16[64,16,128]{2,1,0:T(8,128)(2,1)}, u32[]{:S(2)}, u32[]{:S(2)}) %all-to-all-start.2) | async-done | bytes 262176 | tf_op jit(solution)/shard_map/all_to_all | solution.py:346
  154.8 0.0 copy-done.2
  154.8 1.7 %place.1 = bf16[64,16,128]{2,1,0:T(8,128)(2,1)} custom-call(s32[64]{0:T(128)S(1)} %copy-done.2, bf16[64,16,128]{2,1,0:T(8,128)(2,1)} %all-to-all-done.2.returned_ref), custom_call_target="tpu_custom_call" | custom-call | bytes 524288 | tf_op jit(solution)/shard_map/place/pallas_call | solution.py:243
  (1 shorter events, 0.0 us)
Async XLA Ops:
  3.7 22.2 %copy-start.1 = (bf16[1,128,1024]{2,1,0:T(8,128)(2,1)S(1)}, bf16[1,128,1024]{2,1,0:T(8,128)(2,1)}, u32[]{:S(2)}) copy-start(bf16[1,128,1024]{2,1,0:T(8,128)(2,1)} %param.10) | copy-start | bytes 786436
  3.7 76.3 %all-to-all-start = ((bf16[512,16,128]{2,1,0:T(8,128)(2,1)}), bf16[512,16,128]{2,1,0:T(8,128)(2,1)S(1)}, u32[]{:S(2)}, u32[]{:S(2)}) async-start(bf16[512,16,128]{2,1,0:T(8,128)(2,1)} %bitcast.26), calls=%async_computation | async-start | bytes 4194304 | tf_op jit(solution)/shard_map/all_to_all | solution.py:339
  80.5 36.0 %copy-start.5 = (bf16[1,128,1024]{2,1,0:T(8,128)(2,1)S(1)}, bf16[1,128,1024]{2,1,0:T(8,128)(2,1)}, u32[]{:S(2)}) copy-start(bf16[1,128,1024]{2,1,0:T(8,128)(2,1)} %param.11) | copy-start | bytes 786436
  132.2 0.7 copy-start
  132.9 21.9 %all-to-all-start.2 = ((bf16[64,16,128]{2,1,0:T(8,128)(2,1)}), bf16[64,16,128]{2,1,0:T(8,128)(2,1)}, u32[]{:S(2)}, u32[]{:S(2)}) async-start(bf16[64,16,128]{2,1,0:T(8,128)(2,1)} %bitcast.19), calls=%async_computation.2 | async-start | bytes 524288 | tf_op jit(solution)/shard_map/all_to_all | solution.py:346
  141.8 1.0 copy-start.3
  142.8 1.0 copy-start.4
  143.9 11.0 %copy-start.2 = (s32[64]{0:T(128)S(1)}, s32[64]{0:T(128)}, u32[]{:S(2)}) copy-start(s32[64]{0:T(128)} %assign_ref.3) | copy-start | bytes 772

commit v5 on v4

--- a/solution.py
+++ b/solution.py
@@ -116,13 +116,13 @@
     )(arrived, root)
 
 
-def unpack(spread_ref, k, high, low):
+def unpack(spread_ref, k, high, low, first, count):
     width = spread_ref.shape[2]
     size = high.shape[0]
     rows = size // CODES
     columns = pl.ds(k * width, width)
     scales = scale_of(spread_ref[k, pl.ds(size, CODES), :].astype(jnp.int32).astype(jnp.float32))
-    for g in range(CODES):
+    for g in range(first // rows, (first + count) // rows):
         here = pl.ds(g * rows, rows)
         units = spread_ref[k, here, :].astype(jnp.int32).astype(jnp.float32)
         values = units * scales[g : g + 1]
@@ -131,20 +131,34 @@
         low[here, columns] = (values - upper.astype(jnp.float32)).astype(jnp.bfloat16)
 
 
+def values_of(code):
+    code = code.astype(jnp.int32)
+    count = jnp.abs(code) - 1
+    power = jnp.exp2((1 - lax.shift_right_arithmetic(count, 7)).astype(jnp.float32))
+    value = ((count & 127) + 128).astype(jnp.float32) * (1.0 / 128.0) * power
+    value = jnp.where(code < 0, -value, value)
+    return jnp.where(code == 0, 0.0, value).astype(jnp.bfloat16)
+
+
 def decode(spread_ref, i, left):
-    slabs, rows, size = spread_ref.shape
+    slabs, _, size = spread_ref.shape
+    half = slabs // 2
     start = left.shape[0] + CODES
-    for d in range((rows - start) // size):
-        code = spread_ref[i, pl.ds(start + d * size, size), :].astype(jnp.int32)
-        count = jnp.abs(code) - 1
-        power = jnp.exp2((1 - lax.shift_right_arithmetic(count, 7)).astype(jnp.float32))
-        value = ((count & 127) + 128).astype(jnp.float32) * (1.0 / 128.0) * power
-        value = jnp.where(code < 0, -value, value)
-        value = jnp.where(code == 0, 0.0, value).astype(jnp.bfloat16)
+
+    def at(a, b):
+        return pl.ds(a * size, size), pl.ds(b * size, size)
+
+    for d in range(half):
+        value = values_of(spread_ref[i, pl.ds(start + d * size, size), :])
         j = (i + d) % slabs
-        left[pl.ds(i * size, size), pl.ds(j * size, size)] = value
-        if 0 < d < slabs - d:
-            left[pl.ds(j * size, size), pl.ds(i * size, size)] = value.T
+        left[at(i, j)] = value
+        if d:
+            left[at(j, i)] = value.T
+    if i < half:
+        rest = pl.ds(start + half * size, size // 2)
+        value = values_of(jnp.concatenate([spread_ref[i, rest, :], spread_ref[i + half, rest, :]], axis=0))
+        left[at(i, i + half)] = value
+        left[at(i + half, i)] = value.T
 
 
 NT = (((1,), (1,)), ((), ()))
@@ -167,19 +181,16 @@
     slabs = spread_ref.shape[0]
     size, width = out_ref.shape
     tile = 256
-    for k in range(slabs):
-        unpack(spread_ref, k, high, low)
-        decode(spread_ref, k, left_ref)
-
-    def right_step(t, carry):
-        rows = pl.ds(pl.multiple_of(t * tile, tile), tile)
+    for t in range(size // tile):
+        rows = pl.ds(t * tile, tile)
+        for k in range(slabs):
+            unpack(spread_ref, k, high, low, t * tile, tile)
+        decode(spread_ref, 2 * t, left_ref)
+        decode(spread_ref, 2 * t + 1, left_ref)
         part = dot(high[rows, :], right_ref[...], NT) + dot(low[rows, :], right_ref[...], NT)
         upper = part.astype(jnp.bfloat16)
         mid[rows, pl.ds(0, width)] = upper
         mid[rows, pl.ds(width, width)] = (part - upper.astype(jnp.float32)).astype(jnp.bfloat16)
-        return carry
-
-    lax.fori_loop(0, size // tile, right_step, 0)
 
     square = jnp.zeros((8, width), jnp.float32)
     for t in range(size // tile):
@@ -256,7 +267,7 @@
     rows, size = left_ref.shape
     tile = 256
     for k in range(slabs):
-        unpack(spread_ref, k, high, low)
+        unpack(spread_ref, k, high, low, 0, size)
     own = pl.ds(pl.multiple_of(place_ref[0] * rows, rows), rows)
     turned[pl.ds(0, rows), :] = high[:, own].T
     turned[pl.ds(rows, rows), :] = low[:, own].T
@@ -293,34 +304,44 @@
     )(place, spread, left, right)
 
 
+def codes_of(value):
+    rest = jnp.abs(value)
+    depth = jnp.zeros(value.shape, jnp.float32)
+    for bit in BITS:
+        scaled = rest * (2.0**bit)
+        keep = scaled < 4.0
+        rest = jnp.where(keep, scaled, rest)
+        depth = jnp.where(keep, depth + bit, depth)
+    code = jnp.where(value == 0.0, 0.0, depth * 128.0 + rest * 64.0 - 127.0)
+    return jnp.where(value < 0.0, -code, code).astype(jnp.int32).astype(jnp.int16)
+
+
 def encode_kernel(place_ref, left_ref, code_ref):
     size = left_ref.shape[0]
     slabs = left_ref.shape[1] // size
-    for d in range(code_ref.shape[0] // size):
+    half = slabs // 2
+
+    def block(d):
         column = lax.rem(place_ref[0] + d, slabs) * size
-        value = left_ref[:, pl.ds(pl.multiple_of(column, size), size)].astype(jnp.float32)
-        rest = jnp.abs(value)
-        depth = jnp.zeros(value.shape, jnp.float32)
-        for bit in BITS:
-            scaled = rest * (2.0**bit)
-            keep = scaled < 4.0
-            rest = jnp.where(keep, scaled, rest)
-            depth = jnp.where(keep, depth + bit, depth)
-        code = jnp.where(value == 0.0, 0.0, depth * 128.0 + rest * 64.0 - 127.0)
-        code = jnp.where(value < 0.0, -code, code)
-        code_ref[pl.ds(d * size, size), :] = code.astype(jnp.int32).astype(jnp.int16)
+        return left_ref[:, pl.ds(pl.multiple_of(column, size), size)].astype(jnp.float32)
+
+    for d in range(half):
+        code_ref[pl.ds(d * size, size), :] = codes_of(block(d))
+    last = block(half)
+    last = jnp.where(place_ref[0] < half, last[: size // 2], last.T[size // 2 :])
+    code_ref[pl.ds(half * size, size // 2), :] = codes_of(last)
 
 
 def encode(place, left, slabs):
     rows = left.shape[0]
-    count = slabs // 2 + 1
+    count = slabs * rows // 2 + rows // 2
     return pl.pallas_call(
         encode_kernel,
-        out_shape=jax.ShapeDtypeStruct((count * rows, rows), jnp.int16),
+        out_shape=jax.ShapeDtypeStruct((count, rows), jnp.int16),
         in_specs=[pl.BlockSpec(memory_space=pltpu.SMEM), vmem()],
         out_specs=vmem(),
         compiler_params=pltpu.CompilerParams(vmem_limit_bytes=8 * MIB),
-        cost_estimate=cost(30 * count * rows * rows, 4 * left.size),
+        cost_estimate=cost(30 * count * rows, 4 * left.size),
         name="encode",
     )(place, left)
 

time: 157 us -> 154 us (0.981)
  Pallas kernels: 17.8 us -> 16 us
    pallas_call x1, Pallas kernels: 5.89 us -> 3.95 us  [shape(): pl.pallas_call(shape_kernel, out_shape=(jax.ShapeDtypeStruct((size, width...]
where the time goes in v5:
time: 154 us
  waiting for transfers between devices  58.5 us (38%)
  blocking collectives  44.2 us (29%)
  starting transfers between devices  31.3 us (20%)
  Pallas kernels  16 us (10%)
  local copies, waits for them, and re-layouts  2.79 us (2%)
    all_to_all x1, waiting for transfers between devices, body(): lax.all_to_all(outgoing, ('fsdp', 'dp'), split_axis=0, concat_axis=0, til...  53.5 us
    all_gather x1, blocking collectives, body(): spread = lax.all_gather(packed, 'dp', axis=0)  34.7 us
    all_to_all x1, starting transfers between devices, body(): lax.all_to_all(outgoing, ('fsdp', 'dp'), split_axis=0, concat_axis=0, til...  22.2 us
    all_to_all x1, blocking collectives, body(): lax.all_to_all(squares, 'dp', split_axis=0, concat_axis=0, tiled=True)  9.49 us
    all_to_all x1, starting transfers between devices, body(): lax.all_to_all(rounded, 'fsdp', split_axis=0, concat_axis=0, tiled=True)  9.18 us
    pallas_call x1, Pallas kernels, stats(): pl.pallas_call(stats_kernel, out_shape=(jax.ShapeDtypeStruct(left.shape,...  6.02 us
    all_to_all x1, waiting for transfers between devices, body(): lax.all_to_all(rounded, 'fsdp', split_axis=0, concat_axis=0, tiled=True)  4.96 us
    pallas_call x1, Pallas kernels, shape(): pl.pallas_call(shape_kernel, out_shape=(jax.ShapeDtypeStruct((size, width...  3.95 us
  transfers between devices with their start and end apart: 2, of which 2 were waited for; matrix products, arithmetic and copies ran while one was open for 0% of the time, Pallas kernels for 4%

profile of v5, /device:TPU:1, one launch (start us, length us, event | category | flops | bytes accessed | tf_op | source)
XLA Modules:
  0.0 153.5 jit_solution(11175312932617444540)
XLA Ops:
  0.6 3.0 %send.1 = bf16[64,8,16,128]{3,2,1,0:T(8,128)(2,1)} custom-call(s32[64]{0:T(128)} %assign_ref.3, bf16[64,16,1024]{2,1,0:T(8,128)(2,1)} %bitcast.27), custom_call_target="tpu_custom_call" | custom-call | bytes 4194304 | tf_op jit(solution)/shard_map/send/pallas_call | solution.py:61
  3.7 0.0 copy-start.1
  3.7 22.2 %all-to-all-start = ((bf16[512,16,128]{2,1,0:T(8,128)(2,1)}), bf16[512,16,128]{2,1,0:T(8,128)(2,1)S(1)}, u32[]{:S(2)}, u32[]{:S(2)}) async-start(bf16[512,16,128]{2,1,0:T(8,128)(2,1)} %bitcast.26), calls=%async_computation | async-start | bytes 4194304 | tf_op jit(solution)/shard_map/all_to_all | solution.py:360
  25.9 0.0 copy-done.1
  25.9 0.6 encode.1.root_ref
  26.5 53.5 %all-to-all-done = bf16[512,16,128]{2,1,0:T(8,128)(2,1)S(1)} async-done(((bf16[512,16,128]{2,1,0:T(8,128)(2,1)}), bf16[512,16,128]{2,1,0:T(8,128)(2,1)S(1)}, u32[]{:S(2)}, u32[]{:S(2)}) %all-to-all-start) | async-done | bytes 2097184 | tf_op jit(solution)/shard_map/all_to_all | solution.py:360
  80.0 0.5 fold.1
  80.5 0.0 copy-start.5
  80.5 34.7 %all-gather.2 = s16[12928,128]{1,0:T(8,128)(2,1)S(1)} all-gather(s16[1616,128]{1,0:T(8,128)(2,1)S(1)} %get-tuple-element.15), channel_id=2, replica_groups=mesh['fsdp'=64,'dp'=8] {'dp'}, dimensions={0}, use_global_device_ids=true | all-gather | bytes 3723264 | tf_op jit(solution)/shard_map/all_gather | solution.py:362
  115.3 0.0 copy-done.5
  115.3 3.9 %shape.1 = (f32[1024,128]{1,0:T(8,128)S(1)}, f32[8,128]{1,0:T(8,128)S(1)}) custom-call(s16[8,1616,128]{2,1,0:T(8,128)(2,1)S(1)} %bitcast.17, bf16[128,1024]{1,0:T(8,128)(2,1)S(1)} %bitcast.25, f32[8,128]{1,0:T(8,128)S(1)} %get-tuple-element.16.square_ref), custom_call_target="tpu_custom_call" | custom-call | flops 1073741824 | bytes 6291456 | tf_op jit(solution)/shard_map/shape/pallas_call | solution.py:207
  119.2 9.5 %all_to_all.21 = f32[8,1,128]{2,1,0:T(1,128)S(1)} all-to-all(f32[8,1,128]{2,1,0:T(1,128)S(1)} %bitcast.22), channel_id=1, replica_groups=mesh['fsdp'=64,'dp'=8] {'dp'}, dimensions={0} | all-to-all | bytes 8192 | tf_op jit(solution)/shard_map/all_to_all | solution.py:364
  128.7 0.1 graft.1
  128.9 0.0 copy-start
  128.9 0.7 copy-done
  129.6 9.2 %all-to-all-start.2 = ((bf16[64,16,128]{2,1,0:T(8,128)(2,1)}), bf16[64,16,128]{2,1,0:T(8,128)(2,1)}, u32[]{:S(2)}, u32[]{:S(2)}) async-start(bf16[64,16,128]{2,1,0:T(8,128)(2,1)} %bitcast.19), calls=%async_computation.2 | async-start | bytes 524288 | tf_op jit(solution)/shard_map/all_to_all | solution.py:367
  138.8 0.0 copy-start.3
  138.8 1.0 copy-done.3
  139.8 0.0 copy-start.4
  139.8 1.0 copy-done.4
  140.8 6.0 %stats.1 = (f32[128,1024]{1,0:T(8,128)}, f32[128,1024]{1,0:T(8,128)}) custom-call(s32[1]{0:T(128)} %bitcast.4.place_ref, s16[8,1616,128]{2,1,0:T(8,128)(2,1)S(1)} %bitcast.18, f32[128,1024]{1,0:T(8,128)S(1)} %bitcast.23, f32[128,1024]{1,0:T(8,128)S(1)} %bitcast.24), custom_call_target="tpu_custom_call" | custom-call | flops 1610612736 | bytes 6291456 | tf_op jit(solution)/shard_map/stats/pallas_call | solution.py:291
  146.9 5.0 %all-to-all-done.2.returned_ref = bf16[64,16,128]{2,1,0:T(8,128)(2,1)} async-done(((bf16[64,16,128]{2,1,0:T(8,128)(2,1)}), bf16[64,16,128]{2,1,0:T(8,128)(2,1)}, u32[]{:S(2)}, u32[]{:S(2)}) %all-to-all-start.2) | async-done | bytes 262176 | tf_op jit(solution)/shard_map/all_to_all | solution.py:367
  151.8 0.0 copy-done.2
  151.8 1.7 %place.1 = bf16[64,16,128]{2,1,0:T(8,128)(2,1)} custom-call(s32[64]{0:T(128)S(1)} %copy-done.2, bf16[64,16,128]{2,1,0:T(8,128)(2,1)} %all-to-all-done.2.returned_ref), custom_call_target="tpu_custom_call" | custom-call | bytes 524288 | tf_op jit(solution)/shard_map/place/pallas_call | solution.py:254
  (1 shorter events, 0.0 us)
Async XLA Ops:
  3.7 22.2 %copy-start.1 = (bf16[1,128,1024]{2,1,0:T(8,128)(2,1)S(1)}, bf16[1,128,1024]{2,1,0:T(8,128)(2,1)}, u32[]{:S(2)}) copy-start(bf16[1,128,1024]{2,1,0:T(8,128)(2,1)} %param.10) | copy-start | bytes 786436
  3.7 76.3 %all-to-all-start = ((bf16[512,16,128]{2,1,0:T(8,128)(2,1)}), bf16[512,16,128]{2,1,0:T(8,128)(2,1)S(1)}, u32[]{:S(2)}, u32[]{:S(2)}) async-start(bf16[512,16,128]{2,1,0:T(8,128)(2,1)} %bitcast.26), calls=%async_computation | async-start | bytes 4194304 | tf_op jit(solution)/shard_map/all_to_all | solution.py:360
  80.5 34.8 %copy-start.5 = (bf16[1,128,1024]{2,1,0:T(8,128)(2,1)S(1)}, bf16[1,128,1024]{2,1,0:T(8,128)(2,1)}, u32[]{:S(2)}) copy-start(bf16[1,128,1024]{2,1,0:T(8,128)(2,1)} %param.11) | copy-start | bytes 786436
  128.9 0.7 copy-start
  129.6 22.3 %all-to-all-start.2 = ((bf16[64,16,128]{2,1,0:T(8,128)(2,1)}), bf16[64,16,128]{2,1,0:T(8,128)(2,1)}, u32[]{:S(2)}, u32[]{:S(2)}) async-start(bf16[64,16,128]{2,1,0:T(8,128)(2,1)} %bitcast.19), calls=%async_computation.2 | async-start | bytes 524288 | tf_op jit(solution)/shard_map/all_to_all | solution.py:367
  138.8 1.0 copy-start.3
  139.8 1.0 copy-start.4
  140.8 11.0 %copy-start.2 = (s32[64]{0:T(128)S(1)}, s32[64]{0:T(128)}, u32[]{:S(2)}) copy-start(s32[64]{0:T(128)} %assign_ref.3) | copy-start | bytes 772

commit v6 on v5

--- a/solution.py
+++ b/solution.py
@@ -12,7 +12,8 @@
 STEPS = 90.0
 TOP = 32767.0
 FLOOR = 1e-30
-CODES = 16
+CODES = 8
+HEAD = 16
 BITS = (64, 32, 16, 8, 4, 2, 1)
 MIB = 1 << 20
 
@@ -29,7 +30,7 @@
     return pl.CostEstimate(flops=flops, bytes_accessed=moved, transcendentals=0)
 
 
-def send_kernel(dp_size, assign_ref, grads_ref, out_ref, held, turned, in_sems, out_sem):
+def send_kernel(dp_size, assign_ref, grads_ref, out_ref, owner_of, held, turned, assign_sem, in_sems, out_sem):
     blocks = grads_ref.shape[0]
     col_width = grads_ref.shape[2] // dp_size
     chunks = in_sems.shape[0]
@@ -40,18 +41,17 @@
         )
         for c in range(chunks)
     ]
+    owners = pltpu.make_async_copy(assign_ref, owner_of, assign_sem)
+    owners.start()
     for load in loads:
         load.start()
+    owners.wait()
     for c in range(chunks):
         loads[c].wait()
-
-        def turn(b, carry):
+        for b in range(c * chunk, (c + 1) * chunk):
             for k in range(dp_size):
                 turned[b, k] = held[b, :, pl.ds(k * col_width, col_width)]
-            pltpu.make_async_copy(turned.at[b], out_ref.at[assign_ref[b]], out_sem).start()
-            return carry
-
-        lax.fori_loop(c * chunk, (c + 1) * chunk, turn, 0, unroll=True)
+            pltpu.make_async_copy(turned.at[b], out_ref.at[owner_of[b]], out_sem).start()
     pltpu.make_async_copy(turned, out_ref, out_sem).wait()
 
 
@@ -61,11 +61,13 @@
     return pl.pallas_call(
         functools.partial(send_kernel, dp_size),
         out_shape=jax.ShapeDtypeStruct(shape, grads.dtype),
-        in_specs=[pl.BlockSpec(memory_space=pltpu.SMEM), anywhere()],
+        in_specs=[anywhere()] * 2,
         out_specs=anywhere(),
         scratch_shapes=[
+            pltpu.SMEM((blocks,), jnp.int32),
             pltpu.VMEM(grads.shape, grads.dtype),
             pltpu.VMEM(shape, grads.dtype),
+            pltpu.SemaphoreType.DMA,
             pltpu.SemaphoreType.DMA((8,)),
             pltpu.SemaphoreType.DMA,
         ],
@@ -95,9 +97,11 @@
         codes.append(code)
         square = square + jnp.sum((total * total).reshape(group * rows // 8, 8, width), axis=0)
     square_ref[...] = square
-    codes = jnp.concatenate(codes, axis=0).astype(jnp.int32).astype(jnp.int16)
-    packed_ref[pl.ds(shards * rows, CODES), :] = codes
-    packed_ref[pl.ds(shards * rows + CODES, root_ref.shape[0]), :] = root_ref[...]
+    codes = [code.astype(jnp.int32) for code in codes] + [root_ref[pl.ds(0, HEAD), :].astype(jnp.int32)[CODES:]]
+    size = shards * rows
+    packed_ref[pl.ds(size, HEAD), :] = jnp.concatenate(codes, axis=0).astype(jnp.int16)
+    rest = root_ref.shape[0] - HEAD
+    packed_ref[pl.ds(size + HEAD, rest), :] = root_ref[pl.ds(HEAD, rest), :]
 
 
 def fold(arrived, root):
@@ -105,7 +109,7 @@
     return pl.pallas_call(
         fold_kernel,
         out_shape=(
-            jax.ShapeDtypeStruct((shards * rows + CODES + root.shape[0], width), jnp.int16),
+            jax.ShapeDtypeStruct((shards * rows + root.shape[0], width), jnp.int16),
             jax.ShapeDtypeStruct((8, width), jnp.float32),
         ),
         in_specs=[vmem()] * 2,
@@ -121,7 +125,7 @@
     size = high.shape[0]
     rows = size // CODES
     columns = pl.ds(k * width, width)
-    scales = scale_of(spread_ref[k, pl.ds(size, CODES), :].astype(jnp.int32).astype(jnp.float32))
+    scales = scale_of(spread_ref[k, pl.ds(size, HEAD), :].astype(jnp.int32)[:CODES].astype(jnp.float32))
     for g in range(first // rows, (first + count) // rows):
         here = pl.ds(g * rows, rows)
         units = spread_ref[k, here, :].astype(jnp.int32).astype(jnp.float32)
@@ -137,26 +141,39 @@
     power = jnp.exp2((1 - lax.shift_right_arithmetic(count, 7)).astype(jnp.float32))
     value = ((count & 127) + 128).astype(jnp.float32) * (1.0 / 128.0) * power
     value = jnp.where(code < 0, -value, value)
-    return jnp.where(code == 0, 0.0, value).astype(jnp.bfloat16)
+    return jnp.where(code == 0, 0.0, value)
 
 
 def decode(spread_ref, i, left):
     slabs, _, size = spread_ref.shape
     half = slabs // 2
-    start = left.shape[0] + CODES
+    middle = size // 2
+    head = left.shape[0]
+    start = head + HEAD
 
     def at(a, b):
         return pl.ds(a * size, size), pl.ds(b * size, size)
 
-    for d in range(half):
-        value = values_of(spread_ref[i, pl.ds(start + d * size, size), :])
+    part = values_of(spread_ref[i, pl.ds(start, middle), :])
+    corner = values_of(spread_ref[i, pl.ds(head, HEAD), :].astype(jnp.int32)[CODES : CODES + 1])
+    both = jnp.concatenate([part, pltpu.roll(part, middle, 1)], axis=0)
+    row = lax.broadcasted_iota(jnp.int32, both.shape, 0)
+    lane = lax.broadcasted_iota(jnp.int32, both.shape, 1)
+    direct = ((row < middle) & (row <= lane)) | ((row >= middle) & (lane >= middle) & (row > lane))
+    value = jnp.where(direct, both, both.T)
+    value = jnp.where((row == lane) & (row >= middle), pltpu.roll(corner, middle, 1), value)
+    left[at(i, i)] = value.astype(jnp.bfloat16)
+    start += middle
+    for d in range(1, half):
+        value = values_of(spread_ref[i, pl.ds(start, size), :]).astype(jnp.bfloat16)
         j = (i + d) % slabs
         left[at(i, j)] = value
-        if d:
-            left[at(j, i)] = value.T
+        left[at(j, i)] = value.T
+        start += size
     if i < half:
-        rest = pl.ds(start + half * size, size // 2)
+        rest = pl.ds(start, middle)
         value = values_of(jnp.concatenate([spread_ref[i, rest, :], spread_ref[i + half, rest, :]], axis=0))
+        value = value.astype(jnp.bfloat16)
         left[at(i, i + half)] = value
         left[at(i + half, i)] = value.T
 
@@ -320,21 +337,31 @@
     size = left_ref.shape[0]
     slabs = left_ref.shape[1] // size
     half = slabs // 2
+    middle = size // 2
 
     def block(d):
         column = lax.rem(place_ref[0] + d, slabs) * size
         return left_ref[:, pl.ds(pl.multiple_of(column, size), size)].astype(jnp.float32)
 
-    for d in range(half):
-        code_ref[pl.ds(d * size, size), :] = codes_of(block(d))
+    own = block(0)
+    upper, corner = own[:middle], pltpu.roll(own[middle:], middle, 1)
+    row = lax.broadcasted_iota(jnp.int32, upper.shape, 0)
+    lane = lax.broadcasted_iota(jnp.int32, upper.shape, 1)
+    diagonal = jnp.sum(jnp.where(row == lane, corner, 0.0), axis=0, keepdims=True)
+    code_ref[pl.ds(0, HEAD), :] = codes_of(jnp.broadcast_to(diagonal, (HEAD, size)))
+    code_ref[pl.ds(HEAD, middle), :] = codes_of(jnp.where((lane < middle) & (row > lane), corner, upper))
+    start = HEAD + middle
+    for d in range(1, half):
+        code_ref[pl.ds(start, size), :] = codes_of(block(d))
+        start += size
     last = block(half)
-    last = jnp.where(place_ref[0] < half, last[: size // 2], last.T[size // 2 :])
-    code_ref[pl.ds(half * size, size // 2), :] = codes_of(last)
+    last = jnp.where(place_ref[0] < half, last[:middle], last.T[middle:])
+    code_ref[pl.ds(start, middle), :] = codes_of(last)
 
 
 def encode(place, left, slabs):
     rows = left.shape[0]
-    count = slabs * rows // 2 + rows // 2
+    count = HEAD + slabs * rows // 2
     return pl.pallas_call(
         encode_kernel,
         out_shape=jax.ShapeDtypeStruct((count, rows), jnp.int16),

time: 154 us -> 152 us (0.987)
  no operation moved by 1% of the time
where the time goes in v6:
time: 152 us; the launch traced here: 151 us
  waiting for transfers between devices  58.6 us (39%)
  blocking collectives  42.9 us (28%)
  starting transfers between devices  31.4 us (21%)
  Pallas kernels  15.5 us (10%)
  local copies, waits for them, and re-layouts  2.09 us (1%)
    all_to_all x1, waiting for transfers between devices, body(): lax.all_to_all(outgoing, ('fsdp', 'dp'), split_axis=0, concat_axis=0, til...  53.6 us
    all_gather x1, blocking collectives, body(): spread = lax.all_gather(packed, 'dp', axis=0)  33.3 us
    all_to_all x1, starting transfers between devices, body(): lax.all_to_all(outgoing, ('fsdp', 'dp'), split_axis=0, concat_axis=0, til...  22.2 us
    all_to_all x1, blocking collectives, body(): lax.all_to_all(squares, 'dp', split_axis=0, concat_axis=0, tiled=True)  9.54 us
    all_to_all x1, starting transfers between devices, body(): lax.all_to_all(rounded, 'fsdp', split_axis=0, concat_axis=0, tiled=True)  9.23 us
    pallas_call x1, Pallas kernels, stats(): pl.pallas_call(stats_kernel, out_shape=(jax.ShapeDtypeStruct(left.shape,...  6.11 us
    all_to_all x1, waiting for transfers between devices, body(): lax.all_to_all(rounded, 'fsdp', split_axis=0, concat_axis=0, tiled=True)  4.96 us
    pallas_call x1, Pallas kernels, shape(): pl.pallas_call(shape_kernel, out_shape=(jax.ShapeDtypeStruct((size, width...  3.95 us
  transfers between devices with their start and end apart: 2, of which 2 were waited for; matrix products, arithmetic and copies ran while one was open for 0% of the time, Pallas kernels for 4%

profile of v6, /device:TPU:1, one launch (start us, length us, event | category | flops | bytes accessed | tf_op | source)
XLA Modules:
  0.0 151.2 jit_solution(3108362942486078254)
XLA Ops:
  0.6 2.3 %send.1 = bf16[64,8,16,128]{3,2,1,0:T(8,128)(2,1)} custom-call(s32[64]{0:T(128)} %assign_ref.3, bf16[64,16,1024]{2,1,0:T(8,128)(2,1)} %bitcast.26), custom_call_target="tpu_custom_call" | custom-call | bytes 4194304 | tf_op jit(solution)/shard_map/send/pallas_call | solution.py:61
  3.0 0.0 copy-start
  3.0 22.2 %all-to-all-start = ((bf16[512,16,128]{2,1,0:T(8,128)(2,1)}), bf16[512,16,128]{2,1,0:T(8,128)(2,1)S(1)}, u32[]{:S(2)}, u32[]{:S(2)}) async-start(bf16[512,16,128]{2,1,0:T(8,128)(2,1)} %bitcast.25), calls=%async_computation | async-start | bytes 4194304 | tf_op jit(solution)/shard_map/all_to_all | solution.py:387
  25.2 0.0 copy-done
  25.2 0.5 encode.1.root_ref
  25.7 53.6 %all-to-all-done = bf16[512,16,128]{2,1,0:T(8,128)(2,1)S(1)} async-done(((bf16[512,16,128]{2,1,0:T(8,128)(2,1)}), bf16[512,16,128]{2,1,0:T(8,128)(2,1)S(1)}, u32[]{:S(2)}, u32[]{:S(2)}) %all-to-all-start) | async-done | bytes 2097184 | tf_op jit(solution)/shard_map/all_to_all | solution.py:387
  79.3 0.5 fold.1
  79.8 0.0 copy-start.4
  79.8 33.3 %all-gather.2 = s16[12416,128]{1,0:T(8,128)(2,1)S(1)} all-gather(s16[1552,128]{1,0:T(8,128)(2,1)S(1)} %get-tuple-element.15), channel_id=2, replica_groups=mesh['fsdp'=64,'dp'=8] {'dp'}, dimensions={0}, use_global_device_ids=true | all-gather | bytes 3575808 | tf_op jit(solution)/shard_map/all_gather | solution.py:389
  113.1 0.0 copy-done.4
  113.1 4.0 %shape.1 = (f32[1024,128]{1,0:T(8,128)S(1)}, f32[8,128]{1,0:T(8,128)S(1)}) custom-call(s16[8,1552,128]{2,1,0:T(8,128)(2,1)S(1)} %bitcast.17, bf16[128,1024]{1,0:T(8,128)(2,1)S(1)} %bitcast.24, f32[8,128]{1,0:T(8,128)S(1)} %get-tuple-element.16.square_ref), custom_call_target="tpu_custom_call" | custom-call | flops 1073741824 | bytes 6291456 | tf_op jit(solution)/shard_map/shape/pallas_call | solution.py:224
  117.1 9.5 %all_to_all.21 = f32[8,1,128]{2,1,0:T(1,128)S(1)} all-to-all(f32[8,1,128]{2,1,0:T(1,128)S(1)} %bitcast.21), channel_id=1, replica_groups=mesh['fsdp'=64,'dp'=8] {'dp'}, dimensions={0} | all-to-all | bytes 8192 | tf_op jit(solution)/shard_map/all_to_all | solution.py:391
  126.6 0.8 graft.1
  127.4 9.2 %all-to-all-start.2 = ((bf16[64,16,128]{2,1,0:T(8,128)(2,1)}), bf16[64,16,128]{2,1,0:T(8,128)(2,1)S(1)}, u32[]{:S(2)}, u32[]{:S(2)}) async-start(bf16[64,16,128]{2,1,0:T(8,128)(2,1)} %bitcast.10), calls=%async_computation.2 | async-start | bytes 524288 | tf_op jit(solution)/shard_map/all_to_all | solution.py:394
  136.7 0.0 copy-start.2
  136.7 1.0 copy-done.2
  137.7 0.0 copy-start.3
  137.7 1.0 copy-done.3
  138.8 0.0 copy-start.1
  138.8 6.1 %stats.1 = (f32[128,1024]{1,0:T(8,128)}, f32[128,1024]{1,0:T(8,128)}) custom-call(s32[1]{0:T(128)} %bitcast.4.place_ref, s16[8,1552,128]{2,1,0:T(8,128)(2,1)S(1)} %bitcast.18, f32[128,1024]{1,0:T(8,128)S(1)} %bitcast.22, f32[128,1024]{1,0:T(8,128)S(1)} %bitcast.23), custom_call_target="tpu_custom_call" | custom-call | flops 1610612736 | bytes 6291456 | tf_op jit(solution)/shard_map/stats/pallas_call | solution.py:308
  144.9 5.0 %all-to-all-done.2.returned_ref = bf16[64,16,128]{2,1,0:T(8,128)(2,1)S(1)} async-done(((bf16[64,16,128]{2,1,0:T(8,128)(2,1)}), bf16[64,16,128]{2,1,0:T(8,128)(2,1)S(1)}, u32[]{:S(2)}, u32[]{:S(2)}) %all-to-all-start.2) | async-done | bytes 262176 | tf_op jit(solution)/shard_map/all_to_all | solution.py:394
  149.9 0.0 copy-done.1
  149.9 1.3 place.1
Async XLA Ops:
  3.0 22.2 %copy-start = (bf16[1,128,1024]{2,1,0:T(8,128)(2,1)S(1)}, bf16[1,128,1024]{2,1,0:T(8,128)(2,1)}, u32[]{:S(2)}) copy-start(bf16[1,128,1024]{2,1,0:T(8,128)(2,1)} %param.10) | copy-start | bytes 786436
  3.0 76.3 %all-to-all-start = ((bf16[512,16,128]{2,1,0:T(8,128)(2,1)}), bf16[512,16,128]{2,1,0:T(8,128)(2,1)S(1)}, u32[]{:S(2)}, u32[]{:S(2)}) async-start(bf16[512,16,128]{2,1,0:T(8,128)(2,1)} %bitcast.25), calls=%async_computation | async-start | bytes 4194304 | tf_op jit(solution)/shard_map/all_to_all | solution.py:387
  79.8 33.3 %copy-start.4 = (bf16[1,128,1024]{2,1,0:T(8,128)(2,1)S(1)}, bf16[1,128,1024]{2,1,0:T(8,128)(2,1)}, u32[]{:S(2)}) copy-start(bf16[1,128,1024]{2,1,0:T(8,128)(2,1)} %param.11) | copy-start | bytes 786436
  127.4 22.4 %all-to-all-start.2 = ((bf16[64,16,128]{2,1,0:T(8,128)(2,1)}), bf16[64,16,128]{2,1,0:T(8,128)(2,1)S(1)}, u32[]{:S(2)}, u32[]{:S(2)}) async-start(bf16[64,16,128]{2,1,0:T(8,128)(2,1)} %bitcast.10), calls=%async_computation.2 | async-start | bytes 524288 | tf_op jit(solution)/shard_map/all_to_all | solution.py:394
  136.7 1.0 copy-start.2
  137.7 1.0 copy-start.3
  138.8 11.1 %copy-start.1 = (s32[64]{0:T(128)S(1)}, s32[64]{0:T(128)}, u32[]{:S(2)}) copy-start(s32[64]{0:T(128)} %assign_ref.3) | copy-start | bytes 772

commit v7 on v6

--- a/solution.py
+++ b/solution.py
@@ -137,11 +137,8 @@
 
 def values_of(code):
     code = code.astype(jnp.int32)
-    count = jnp.abs(code) - 1
-    power = jnp.exp2((1 - lax.shift_right_arithmetic(count, 7)).astype(jnp.float32))
-    value = ((count & 127) + 128).astype(jnp.float32) * (1.0 / 128.0) * power
-    value = jnp.where(code < 0, -value, value)
-    return jnp.where(code == 0, 0.0, value)
+    power = jnp.exp2((1 - (code & 127)).astype(jnp.float32))
+    return lax.shift_right_arithmetic(code, 7).astype(jnp.float32) * (1.0 / 128.0) * power
 
 
 def decode(spread_ref, i, left):
@@ -197,13 +194,13 @@
 def shape_kernel(spread_ref, right_ref, square_ref, out_ref, squares_ref, high, low, mid, left_ref):
     slabs = spread_ref.shape[0]
     size, width = out_ref.shape
-    tile = 256
+    tile = 512
     for t in range(size // tile):
         rows = pl.ds(t * tile, tile)
         for k in range(slabs):
             unpack(spread_ref, k, high, low, t * tile, tile)
-        decode(spread_ref, 2 * t, left_ref)
-        decode(spread_ref, 2 * t + 1, left_ref)
+        for i in range(4 * t, 4 * t + 4):
+            decode(spread_ref, i, left_ref)
         part = dot(high[rows, :], right_ref[...], NT) + dot(low[rows, :], right_ref[...], NT)
         upper = part.astype(jnp.bfloat16)
         mid[rows, pl.ds(0, width)] = upper
@@ -283,24 +280,22 @@
     slabs = spread_ref.shape[0]
     rows, size = left_ref.shape
     tile = 256
-    for k in range(slabs):
-        unpack(spread_ref, k, high, low, 0, size)
+    for t in range(size // tile):
+        for k in range(slabs):
+            unpack(spread_ref, k, high, low, t * tile, tile)
     own = pl.ds(pl.multiple_of(place_ref[0] * rows, rows), rows)
     turned[pl.ds(0, rows), :] = high[:, own].T
     turned[pl.ds(rows, rows), :] = low[:, own].T
 
-    def step(t, carry):
-        here = pl.ds(pl.multiple_of(t * tile, tile), tile)
-        part = dot(high[own, :], high[here, :], NT)
-        part += dot(low[own, :], high[here, :], NT)
-        part += dot(high[own, :], low[here, :], NT)
-        left_out[:, here] = DECAY_RATE * left_ref[:, here] + (1.0 - DECAY_RATE) * part
+    mine = jnp.concatenate([high[own, :], low[own, :]], axis=0)
+    for t in range(size // tile):
+        here = pl.ds(t * tile, tile)
+        both = dot(high[here, :], mine, NT)
+        part = both[:, :rows] + both[:, rows:] + dot(low[here, :], mine[:rows], NT)
+        left_out[:, here] = DECAY_RATE * left_ref[:, here] + (1.0 - DECAY_RATE) * part.T
         both = dot(turned[...], high[:, here], NN)
         part = both[:rows] + both[rows:] + dot(turned[pl.ds(0, rows), :], low[:, here], NN)
         right_out[:, here] = DECAY_RATE * right_ref[:, here] + (1.0 - DECAY_RATE) * part
-        return carry
-
-    lax.fori_loop(0, size // tile, step, 0)
 
 
 def stats(place, spread, left, right):
@@ -329,8 +324,8 @@
         keep = scaled < 4.0
         rest = jnp.where(keep, scaled, rest)
         depth = jnp.where(keep, depth + bit, depth)
-    code = jnp.where(value == 0.0, 0.0, depth * 128.0 + rest * 64.0 - 127.0)
-    return jnp.where(value < 0.0, -code, code).astype(jnp.int32).astype(jnp.int16)
+    fraction = jnp.where(value < 0.0, -rest, rest) * 64.0
+    return (fraction * 128.0 + depth).astype(jnp.int32).astype(jnp.int16)
 
 
 def encode_kernel(place_ref, left_ref, code_ref):

time: 152 us -> 151 us (level)
  Pallas kernels: 15.5 us -> 13.4 us
  transfers between devices with their start and end apart: 2 -> 2, of which waited for: 2 -> 2; matrix products, arithmetic and copies ran while one was open for 0% -> 0% of each run, Pallas kernels for 4% -> 3%
where the time goes in v7:
time: 151 us; the launch traced here: 150 us
  waiting for transfers between devices  60 us (40%)
  blocking collectives  42.9 us (28%)
  starting transfers between devices  31.4 us (21%)
  Pallas kernels  13.4 us (9%)
  local copies, waits for them, and re-layouts  2.09 us (1%)
    all_to_all x1, waiting for transfers between devices, body(): lax.all_to_all(outgoing, ('fsdp', 'dp'), split_axis=0, concat_axis=0, til...  53.6 us
    all_gather x1, blocking collectives, body(): spread = lax.all_gather(packed, 'dp', axis=0)  33.3 us
    all_to_all x1, starting transfers between devices, body(): lax.all_to_all(outgoing, ('fsdp', 'dp'), split_axis=0, concat_axis=0, til...  22.2 us
    all_to_all x1, blocking collectives, body(): lax.all_to_all(squares, 'dp', split_axis=0, concat_axis=0, tiled=True)  9.54 us
    all_to_all x1, starting transfers between devices, body(): lax.all_to_all(rounded, 'fsdp', split_axis=0, concat_axis=0, tiled=True)  9.23 us
    all_to_all x1, waiting for transfers between devices, body(): lax.all_to_all(rounded, 'fsdp', split_axis=0, concat_axis=0, tiled=True)  6.35 us
    pallas_call x1, Pallas kernels, stats(): pl.pallas_call(stats_kernel, out_shape=(jax.ShapeDtypeStruct(left.shape,...  4.72 us
    pallas_call x1, Pallas kernels, shape(): pl.pallas_call(shape_kernel, out_shape=(jax.ShapeDtypeStruct((size, width...  3.23 us
  transfers between devices with their start and end apart: 2, of which 2 were waited for; matrix products, arithmetic and copies ran while one was open for 0% of the time, Pallas kernels for 3%

profile of v7, /device:TPU:1, one launch (start us, length us, event | category | flops | bytes accessed | tf_op | source)
XLA Modules:
  0.0 150.5 jit_solution(2768011088167371040)
XLA Ops:
  0.6 2.4 %send.1 = bf16[64,8,16,128]{3,2,1,0:T(8,128)(2,1)} custom-call(s32[64]{0:T(128)} %assign_ref.3, bf16[64,16,1024]{2,1,0:T(8,128)(2,1)} %bitcast.26), custom_call_target="tpu_custom_call" | custom-call | bytes 4194304 | tf_op jit(solution)/shard_map/send/pallas_call | solution.py:61
  3.0 0.0 copy-start
  3.0 22.2 %all-to-all-start = ((bf16[512,16,128]{2,1,0:T(8,128)(2,1)}), bf16[512,16,128]{2,1,0:T(8,128)(2,1)S(1)}, u32[]{:S(2)}, u32[]{:S(2)}) async-start(bf16[512,16,128]{2,1,0:T(8,128)(2,1)} %bitcast.25), calls=%async_computation | async-start | bytes 4194304 | tf_op jit(solution)/shard_map/all_to_all | solution.py:382
  25.2 0.0 copy-done
  25.2 0.5 encode.1.root_ref
  25.7 53.6 %all-to-all-done = bf16[512,16,128]{2,1,0:T(8,128)(2,1)S(1)} async-done(((bf16[512,16,128]{2,1,0:T(8,128)(2,1)}), bf16[512,16,128]{2,1,0:T(8,128)(2,1)S(1)}, u32[]{:S(2)}, u32[]{:S(2)}) %all-to-all-start) | async-done | bytes 2097184 | tf_op jit(solution)/shard_map/all_to_all | solution.py:382
  79.3 0.5 fold.1
  79.8 0.0 copy-start.4
  79.8 33.3 %all-gather.2 = s16[12416,128]{1,0:T(8,128)(2,1)S(1)} all-gather(s16[1552,128]{1,0:T(8,128)(2,1)S(1)} %get-tuple-element.15), channel_id=2, replica_groups=mesh['fsdp'=64,'dp'=8] {'dp'}, dimensions={0}, use_global_device_ids=true | all-gather | bytes 3575808 | tf_op jit(solution)/shard_map/all_gather | solution.py:384
  113.2 0.0 copy-done.4
  113.2 3.2 %shape.1 = (f32[1024,128]{1,0:T(8,128)S(1)}, f32[8,128]{1,0:T(8,128)S(1)}) custom-call(s16[8,1552,128]{2,1,0:T(8,128)(2,1)S(1)} %bitcast.17, bf16[128,1024]{1,0:T(8,128)(2,1)S(1)} %bitcast.24, f32[8,128]{1,0:T(8,128)S(1)} %get-tuple-element.16.square_ref), custom_call_target="tpu_custom_call" | custom-call | flops 1073741824 | bytes 6291456 | tf_op jit(solution)/shard_map/shape/pallas_call | solution.py:221
  116.4 9.5 %all_to_all.21 = f32[8,1,128]{2,1,0:T(1,128)S(1)} all-to-all(f32[8,1,128]{2,1,0:T(1,128)S(1)} %bitcast.21), channel_id=1, replica_groups=mesh['fsdp'=64,'dp'=8] {'dp'}, dimensions={0} | all-to-all | bytes 8192 | tf_op jit(solution)/shard_map/all_to_all | solution.py:386
  125.9 0.8 graft.1
  126.8 9.2 %all-to-all-start.2 = ((bf16[64,16,128]{2,1,0:T(8,128)(2,1)}), bf16[64,16,128]{2,1,0:T(8,128)(2,1)S(1)}, u32[]{:S(2)}, u32[]{:S(2)}) async-start(bf16[64,16,128]{2,1,0:T(8,128)(2,1)} %bitcast.10), calls=%async_computation.2 | async-start | bytes 524288 | tf_op jit(solution)/shard_map/all_to_all | solution.py:389
  136.0 0.0 copy-start.2
  136.0 1.0 copy-done.2
  137.1 0.0 copy-start.3
  137.1 1.0 copy-done.3
  138.1 0.0 copy-start.1
  138.1 4.7 %stats.1 = (f32[128,1024]{1,0:T(8,128)}, f32[128,1024]{1,0:T(8,128)}) custom-call(s32[1]{0:T(128)} %bitcast.4.place_ref, s16[8,1552,128]{2,1,0:T(8,128)(2,1)S(1)} %bitcast.18, f32[128,1024]{1,0:T(8,128)S(1)} %bitcast.22, f32[128,1024]{1,0:T(8,128)S(1)} %bitcast.23), custom_call_target="tpu_custom_call" | custom-call | flops 1610612736 | bytes 6291456 | tf_op jit(solution)/shard_map/stats/pallas_call | solution.py:303
  142.8 6.3 %all-to-all-done.2.returned_ref = bf16[64,16,128]{2,1,0:T(8,128)(2,1)S(1)} async-done(((bf16[64,16,128]{2,1,0:T(8,128)(2,1)}), bf16[64,16,128]{2,1,0:T(8,128)(2,1)S(1)}, u32[]{:S(2)}, u32[]{:S(2)}) %all-to-all-start.2) | async-done | bytes 262176 | tf_op jit(solution)/shard_map/all_to_all | solution.py:389
  149.2 0.0 copy-done.1
  149.2 1.3 place.1
Async XLA Ops:
  3.0 22.2 %copy-start = (bf16[1,128,1024]{2,1,0:T(8,128)(2,1)S(1)}, bf16[1,128,1024]{2,1,0:T(8,128)(2,1)}, u32[]{:S(2)}) copy-start(bf16[1,128,1024]{2,1,0:T(8,128)(2,1)} %param.10) | copy-start | bytes 786436
  3.0 76.3 %all-to-all-start = ((bf16[512,16,128]{2,1,0:T(8,128)(2,1)}), bf16[512,16,128]{2,1,0:T(8,128)(2,1)S(1)}, u32[]{:S(2)}, u32[]{:S(2)}) async-start(bf16[512,16,128]{2,1,0:T(8,128)(2,1)} %bitcast.25), calls=%async_computation | async-start | bytes 4194304 | tf_op jit(solution)/shard_map/all_to_all | solution.py:382
  79.8 33.3 %copy-start.4 = (bf16[1,128,1024]{2,1,0:T(8,128)(2,1)S(1)}, bf16[1,128,1024]{2,1,0:T(8,128)(2,1)}, u32[]{:S(2)}) copy-start(bf16[1,128,1024]{2,1,0:T(8,128)(2,1)} %param.11) | copy-start | bytes 786436
  126.8 22.4 %all-to-all-start.2 = ((bf16[64,16,128]{2,1,0:T(8,128)(2,1)}), bf16[64,16,128]{2,1,0:T(8,128)(2,1)S(1)}, u32[]{:S(2)}, u32[]{:S(2)}) async-start(bf16[64,16,128]{2,1,0:T(8,128)(2,1)} %bitcast.10), calls=%async_computation.2 | async-start | bytes 524288 | tf_op jit(solution)/shard_map/all_to_all | solution.py:389
  136.0 1.0 copy-start.2
  137.1 1.0 copy-start.3
  138.1 11.1 %copy-start.1 = (s32[64]{0:T(128)S(1)}, s32[64]{0:T(128)}, u32[]{:S(2)}) copy-start(s32[64]{0:T(128)} %assign_ref.3) | copy-start | bytes 772

commit v8 on v7

--- a/solution.py
+++ b/solution.py
@@ -120,19 +120,22 @@
     )(arrived, root)
 
 
+def halves_of(spread_ref, k, size, first, count):
+    rows = size // CODES
+    scales = scale_of(spread_ref[k, pl.ds(size, HEAD), :].astype(jnp.int32)[:CODES].astype(jnp.float32))
+    upper, lower = [], []
+    for g in range(first // rows, (first + count) // rows):
+        units = spread_ref[k, pl.ds(g * rows, rows), :].astype(jnp.int32).astype(jnp.float32)
+        values = units * scales[g : g + 1]
+        upper.append(values.astype(jnp.bfloat16))
+        lower.append((values - upper[-1].astype(jnp.float32)).astype(jnp.bfloat16))
+    return jnp.concatenate(upper, axis=0), jnp.concatenate(lower, axis=0)
+
+
 def unpack(spread_ref, k, high, low, first, count):
     width = spread_ref.shape[2]
-    size = high.shape[0]
-    rows = size // CODES
-    columns = pl.ds(k * width, width)
-    scales = scale_of(spread_ref[k, pl.ds(size, HEAD), :].astype(jnp.int32)[:CODES].astype(jnp.float32))
-    for g in range(first // rows, (first + count) // rows):
-        here = pl.ds(g * rows, rows)
-        units = spread_ref[k, here, :].astype(jnp.int32).astype(jnp.float32)
-        values = units * scales[g : g + 1]
-        upper = values.astype(jnp.bfloat16)
-        high[here, columns] = upper
-        low[here, columns] = (values - upper.astype(jnp.float32)).astype(jnp.bfloat16)
+    here = pl.ds(first, count), pl.ds(k * width, width)
+    high[here], low[here] = halves_of(spread_ref, k, high.shape[0], first, count)
 
 
 def values_of(code):
@@ -191,17 +194,17 @@
     return jnp.where(lane < width // 2, a, b)
 
 
-def shape_kernel(spread_ref, right_ref, square_ref, out_ref, squares_ref, high, low, mid, left_ref):
+def shape_kernel(spread_ref, right_ref, square_ref, out_ref, squares_ref, mid, left_ref):
     slabs = spread_ref.shape[0]
     size, width = out_ref.shape
-    tile = 512
+    tile = 256
     for t in range(size // tile):
         rows = pl.ds(t * tile, tile)
-        for k in range(slabs):
-            unpack(spread_ref, k, high, low, t * tile, tile)
-        for i in range(4 * t, 4 * t + 4):
+        pairs = [halves_of(spread_ref, k, size, t * tile, tile) for k in range(slabs)]
+        upper, lower = (jnp.concatenate(terms, axis=1) for terms in zip(*pairs))
+        for i in range(2 * t, 2 * t + 2):
             decode(spread_ref, i, left_ref)
-        part = dot(high[rows, :], right_ref[...], NT) + dot(low[rows, :], right_ref[...], NT)
+        part = dot(upper, right_ref[...], NT) + dot(lower, right_ref[...], NT)
         upper = part.astype(jnp.bfloat16)
         mid[rows, pl.ds(0, width)] = upper
         mid[rows, pl.ds(width, width)] = (part - upper.astype(jnp.float32)).astype(jnp.bfloat16)
@@ -227,8 +230,6 @@
         in_specs=[vmem()] * 3,
         out_specs=(vmem(),) * 2,
         scratch_shapes=[
-            pltpu.VMEM((size, size), jnp.bfloat16),
-            pltpu.VMEM((size, size), jnp.bfloat16),
             pltpu.VMEM((size, 2 * width), jnp.bfloat16),
             pltpu.VMEM((size, size), jnp.bfloat16),
         ],

time: 151 us -> 150 us (level)
  transfers between devices with their start and end apart: 2 -> 2, of which waited for: 2 -> 2; matrix products, arithmetic and copies ran while one was open for 0% -> 0% of each run, Pallas kernels for 3% -> 4%
where the time goes in v8:
time: 150 us
  waiting for transfers between devices  59.9 us (40%)
  blocking collectives  42.9 us (29%)
  starting transfers between devices  31.4 us (21%)
  Pallas kernels  12.8 us (9%)
  local copies, waits for them, and re-layouts  2.09 us (1%)
    all_to_all x1, waiting for transfers between devices, body(): lax.all_to_all(outgoing, ('fsdp', 'dp'), split_axis=0, concat_axis=0, til...  53.6 us
    all_gather x1, blocking collectives, body(): spread = lax.all_gather(packed, 'dp', axis=0)  33.3 us
    all_to_all x1, starting transfers between devices, body(): lax.all_to_all(outgoing, ('fsdp', 'dp'), split_axis=0, concat_axis=0, til...  22.2 us
    all_to_all x1, blocking collectives, body(): lax.all_to_all(squares, 'dp', split_axis=0, concat_axis=0, tiled=True)  9.53 us
    all_to_all x1, starting transfers between devices, body(): lax.all_to_all(rounded, 'fsdp', split_axis=0, concat_axis=0, tiled=True)  9.23 us
    all_to_all x1, waiting for transfers between devices, body(): lax.all_to_all(rounded, 'fsdp', split_axis=0, concat_axis=0, tiled=True)  6.29 us
    pallas_call x1, Pallas kernels, stats(): pl.pallas_call(stats_kernel, out_shape=(jax.ShapeDtypeStruct(left.shape,...  4.78 us
  transfers between devices with their start and end apart: 2, of which 2 were waited for; matrix products, arithmetic and copies ran while one was open for 0% of the time, Pallas kernels for 4%

profile of v8, /device:TPU:1, one launch (start us, length us, event | category | flops | bytes accessed | tf_op | source)
XLA Modules:
  0.0 149.8 jit_solution(274643341063226353)
XLA Ops:
  0.6 2.4 %send.1 = bf16[64,8,16,128]{3,2,1,0:T(8,128)(2,1)} custom-call(s32[64]{0:T(128)} %assign_ref.3, bf16[64,16,1024]{2,1,0:T(8,128)(2,1)} %bitcast.26), custom_call_target="tpu_custom_call" | custom-call | bytes 4194304 | tf_op jit(solution)/shard_map/send/pallas_call | solution.py:61
  3.0 0.0 copy-start
  3.0 22.2 %all-to-all-start = ((bf16[512,16,128]{2,1,0:T(8,128)(2,1)}), bf16[512,16,128]{2,1,0:T(8,128)(2,1)S(1)}, u32[]{:S(2)}, u32[]{:S(2)}) async-start(bf16[512,16,128]{2,1,0:T(8,128)(2,1)} %bitcast.25), calls=%async_computation | async-start | bytes 4194304 | tf_op jit(solution)/shard_map/all_to_all | solution.py:383
  25.2 0.0 copy-done
  25.2 0.5 encode.1.root_ref
  25.7 53.6 %all-to-all-done = bf16[512,16,128]{2,1,0:T(8,128)(2,1)S(1)} async-done(((bf16[512,16,128]{2,1,0:T(8,128)(2,1)}), bf16[512,16,128]{2,1,0:T(8,128)(2,1)S(1)}, u32[]{:S(2)}, u32[]{:S(2)}) %all-to-all-start) | async-done | bytes 2097184 | tf_op jit(solution)/shard_map/all_to_all | solution.py:383
  79.3 0.5 fold.1
  79.8 0.0 copy-start.4
  79.8 33.3 %all-gather.2 = s16[12416,128]{1,0:T(8,128)(2,1)S(1)} all-gather(s16[1552,128]{1,0:T(8,128)(2,1)S(1)} %get-tuple-element.15), channel_id=2, replica_groups=mesh['fsdp'=64,'dp'=8] {'dp'}, dimensions={0}, use_global_device_ids=true | all-gather | bytes 3575808 | tf_op jit(solution)/shard_map/all_gather | solution.py:385
  113.1 0.0 copy-done.4
  113.1 2.6 %shape.1 = (f32[1024,128]{1,0:T(8,128)S(1)}, f32[8,128]{1,0:T(8,128)S(1)}) custom-call(s16[8,1552,128]{2,1,0:T(8,128)(2,1)S(1)} %bitcast.17, bf16[128,1024]{1,0:T(8,128)(2,1)S(1)} %bitcast.24, f32[8,128]{1,0:T(8,128)S(1)} %get-tuple-element.16.square_ref), custom_call_target="tpu_custom_call" | custom-call | flops 1073741824 | bytes 6291456 | tf_op jit(solution)/shard_map/shape/pallas_call | solution.py:224
  115.7 9.5 %all_to_all.21 = f32[8,1,128]{2,1,0:T(1,128)S(1)} all-to-all(f32[8,1,128]{2,1,0:T(1,128)S(1)} %bitcast.21), channel_id=1, replica_groups=mesh['fsdp'=64,'dp'=8] {'dp'}, dimensions={0} | all-to-all | bytes 8192 | tf_op jit(solution)/shard_map/all_to_all | solution.py:387
  125.3 0.8 graft.1
  126.1 9.2 %all-to-all-start.2 = ((bf16[64,16,128]{2,1,0:T(8,128)(2,1)}), bf16[64,16,128]{2,1,0:T(8,128)(2,1)S(1)}, u32[]{:S(2)}, u32[]{:S(2)}) async-start(bf16[64,16,128]{2,1,0:T(8,128)(2,1)} %bitcast.10), calls=%async_computation.2 | async-start | bytes 524288 | tf_op jit(solution)/shard_map/all_to_all | solution.py:390
  135.4 0.0 copy-start.2
  135.4 1.0 copy-done.2
  136.4 0.0 copy-start.3
  136.4 1.0 copy-done.3
  137.5 0.0 copy-start.1
  137.5 4.8 %stats.1 = (f32[128,1024]{1,0:T(8,128)}, f32[128,1024]{1,0:T(8,128)}) custom-call(s32[1]{0:T(128)} %bitcast.4.place_ref, s16[8,1552,128]{2,1,0:T(8,128)(2,1)S(1)} %bitcast.18, f32[128,1024]{1,0:T(8,128)S(1)} %bitcast.22, f32[128,1024]{1,0:T(8,128)S(1)} %bitcast.23), custom_call_target="tpu_custom_call" | custom-call | flops 1610612736 | bytes 6291456 | tf_op jit(solution)/shard_map/stats/pallas_call | solution.py:304
  142.2 6.3 %all-to-all-done.2.returned_ref = bf16[64,16,128]{2,1,0:T(8,128)(2,1)S(1)} async-done(((bf16[64,16,128]{2,1,0:T(8,128)(2,1)}), bf16[64,16,128]{2,1,0:T(8,128)(2,1)S(1)}, u32[]{:S(2)}, u32[]{:S(2)}) %all-to-all-start.2) | async-done | bytes 262176 | tf_op jit(solution)/shard_map/all_to_all | solution.py:390
  148.5 0.0 copy-done.1
  148.5 1.3 place.1
Async XLA Ops:
  3.0 22.2 %copy-start = (bf16[1,128,1024]{2,1,0:T(8,128)(2,1)S(1)}, bf16[1,128,1024]{2,1,0:T(8,128)(2,1)}, u32[]{:S(2)}) copy-start(bf16[1,128,1024]{2,1,0:T(8,128)(2,1)} %param.10) | copy-start | bytes 786436
  3.0 76.3 %all-to-all-start = ((bf16[512,16,128]{2,1,0:T(8,128)(2,1)}), bf16[512,16,128]{2,1,0:T(8,128)(2,1)S(1)}, u32[]{:S(2)}, u32[]{:S(2)}) async-start(bf16[512,16,128]{2,1,0:T(8,128)(2,1)} %bitcast.25), calls=%async_computation | async-start | bytes 4194304 | tf_op jit(solution)/shard_map/all_to_all | solution.py:383
  79.8 33.3 %copy-start.4 = (bf16[1,128,1024]{2,1,0:T(8,128)(2,1)S(1)}, bf16[1,128,1024]{2,1,0:T(8,128)(2,1)}, u32[]{:S(2)}) copy-start(bf16[1,128,1024]{2,1,0:T(8,128)(2,1)} %param.11) | copy-start | bytes 786436
  126.1 22.4 %all-to-all-start.2 = ((bf16[64,16,128]{2,1,0:T(8,128)(2,1)}), bf16[64,16,128]{2,1,0:T(8,128)(2,1)S(1)}, u32[]{:S(2)}, u32[]{:S(2)}) async-start(bf16[64,16,128]{2,1,0:T(8,128)(2,1)} %bitcast.10), calls=%async_computation.2 | async-start | bytes 524288 | tf_op jit(solution)/shard_map/all_to_all | solution.py:390
  135.4 1.0 copy-start.2
  136.4 1.0 copy-start.3
  137.5 11.1 %copy-start.1 = (s32[64]{0:T(128)S(1)}, s32[64]{0:T(128)}, u32[]{:S(2)}) copy-start(s32[64]{0:T(128)} %assign_ref.3) | copy-start | bytes 772
